TPU v7x, 32 devices: a whole 2x2x4 slice. The times are simulated.
32 devices in a mesh: depth: 4 (over y, x), row: 2 (over core), col: 4 (over z).
Axes of the slice: x: 2, y: 2, z: 4, core: 2. Of those that a mesh axis runs over, the one named last changes fastest.
Arguments:
- species: float32 [2, 64, 64, 512], P(None, 'depth', 'row', 'col'), may hold values from -6 to 6
- diffusivity: float32 [64, 64, 512], P('depth', 'row', 'col'), may hold values from 0.05 to 0.4
- reaction_rate: float32 [64, 64, 512], P('depth', 'row', 'col'), may hold values from 0.2 to 2
- shear_rate: float32 [16], replicated, may hold values from -0.08 to 0.08
- colour_weight: float32 [16, 4, 2], replicated, may hold values from -4 to 4
- colour_bias: float32 [16, 4], replicated, may hold values from -1 to 1
- slab_order: int32 [16, 4], replicated, may hold values from 0 to 3, each once within a row
- lengths: int32 [16, 4, 64], P('depth', 'col', 'row'), may hold values from 1 to 128
- owners: int32 [16, 4, 64, 1], P('depth', 'col', 'row'), may hold values from 0 to 3; in each aligned block of 32 rows (0 to 31, 32 to 63, ..., all dimensions but the last counted through in order) at most 16 rows name the same one
- warp_matrix: bfloat16 [16, 128, 128], replicated, may hold values from -0.5 to 0.5
Outputs:
- species_out: float32 [2, 64, 64, 512], P(None, 'depth', 'row', 'col')
- frame: float32 [16, 64, 4, 512], P('depth', 'row', None, 'col')
Inputs may be any that keep to these rules, and one draw needn't show every extreme that they name: `slab_order`: each row names each of the 4 slabs once. `owners`: for one view, the 32 scanlines of one device (aligned blocks of 32 along the third dimension) name any one owner at most 16 times.
All inputs are finite; a program needn't handle non-finite values.
Results may differ from a plain program's by a relative error of at most 0.001.
The roundings to bfloat16 on the way count: a program that leaves them out, or rounds other values in their place, can miss the bound.
Values may be sent and summed in bfloat16 or wider, within the bound.
A program may use at most 64 MiB of HBM per device.

v0:
```python
import jax
import jax.numpy as jnp
from jax import lax
from jax.sharding import PartitionSpec as P

TIME_STEP = 0.1
RAY_STEP = 0.02
VEL_DEPTH = 0.3
VEL_ROW = 0.2
VEL_COL = 0.4


def with_halo(cells, sides, width):
    for axis, dim in sides:
        count = lax.axis_size(axis)
        ends = count - 1
        head = lax.slice_in_dim(cells, 0, width, axis=dim)
        tail = lax.slice_in_dim(cells, cells.shape[dim] - width, cells.shape[dim], axis=dim)
        cells = jnp.concatenate(
            [
                lax.ppermute(tail, axis, [(i, (i + 1) % count) for i in range(ends)]),
                cells,
                lax.ppermute(head, axis, [((i + 1) % count, i) for i in range(ends)]),
            ],
            axis=dim,
        )
    return cells


def tendency_of(padded, diffusivity, reaction_rate):
    centre = padded[:, 1:-1, 1:-1, 1:-1]
    below_depth = padded[:, :-2, 1:-1, 1:-1]
    above_depth = padded[:, 2:, 1:-1, 1:-1]
    below_row = padded[:, 1:-1, :-2, 1:-1]
    above_row = padded[:, 1:-1, 2:, 1:-1]
    below_col = padded[:, 1:-1, 1:-1, :-2]
    above_col = padded[:, 1:-1, 1:-1, 2:]
    laplace = (
        below_depth + above_depth + below_row + above_row + below_col + above_col - 6.0 * centre
    )
    advect = (
        VEL_DEPTH * (centre - below_depth)
        + VEL_ROW * (centre - below_row)
        + VEL_COL * (centre - below_col)
    )
    heat_part = centre[1]
    burned = reaction_rate * centre[0] * heat_part * heat_part / (1.0 + heat_part * heat_part)
    source = jnp.stack([-burned, burned])
    return diffusivity * laplace - advect + source


def trimmed(array, layers):
    depth_len = array.shape[-3]
    row_len = array.shape[-2]
    col_len = array.shape[-1]
    return array[
        ..., layers : depth_len - layers, layers : row_len - layers, layers : col_len - layers
    ]


def inside_grid(first_index, count, margin, total):
    places = first_index - margin + jnp.arange(count + 2 * margin, dtype=jnp.int32)
    return (places >= 0) & (places < total)


def advance_deep(species, diffusivity, reaction_rate, rim_width):
    depth_cells = species.shape[1]
    rows = species.shape[2]
    width = species.shape[3]
    packed = jnp.concatenate([species, diffusivity[None], reaction_rate[None]], axis=0)
    wide = with_halo(packed, (("col", 3),), 3 + rim_width)
    deep = with_halo(wide, (("depth", 1), ("row", 2)), 3)
    depth_ok = inside_grid(
        lax.axis_index("depth") * depth_cells, depth_cells, 3, depth_cells * lax.axis_size("depth")
    )
    row_ok = inside_grid(lax.axis_index("row") * rows, rows, 3, rows * lax.axis_size("row"))
    col_ok = inside_grid(
        lax.axis_index("col") * width, width, 3 + rim_width, width * lax.axis_size("col")
    )
    inside = depth_ok[:, None, None] & row_ok[None, :, None] & col_ok[None, None, :]
    fields = deep[:2]
    spread = deep[2]
    rates = deep[3]
    zero = jnp.zeros((), jnp.float32)
    first = trimmed(fields, 1) + TIME_STEP * tendency_of(
        fields, trimmed(spread, 1), trimmed(rates, 1)
    )
    first = jnp.where(trimmed(inside, 1)[None], first, zero)
    second = 0.75 * trimmed(fields, 2) + 0.25 * (
        trimmed(first, 1) + TIME_STEP * tendency_of(first, trimmed(spread, 2), trimmed(rates, 2))
    )
    second = jnp.where(trimmed(inside, 2)[None], second, zero)
    final = trimmed(fields, 3) / 3.0 + 2.0 / 3.0 * (
        trimmed(second, 1) + TIME_STEP * tendency_of(second, trimmed(spread, 3), trimmed(rates, 3))
    )
    final = jnp.where(trimmed(inside, 3)[None], final, zero)
    return final


def slot_plan(owner_rows, tiles):
    onehot = (owner_rows[..., None] == jnp.arange(tiles, dtype=jnp.int32)).astype(jnp.int32)
    running = jnp.cumsum(onehot, axis=-2)
    return jnp.sum(running * onehot, axis=-1) - 1


def body(
    species,
    diffusivity,
    reaction_rate,
    shear_rate,
    colour_weight,
    colour_bias,
    slab_order,
    lengths,
    owners,
    warp_matrix,
):
    depth_cells = species.shape[1]
    rows = species.shape[2]
    width = species.shape[3]
    depth_devices = lax.axis_size("depth")
    depth_total = depth_cells * depth_devices
    rim_width = (4 * depth_total + 99) // 100
    rimmed = advance_deep(species, diffusivity, reaction_rate, rim_width)
    species_out = rimmed[:, :, :, rim_width : rim_width + width]
    slab_first = lax.axis_index("depth") * depth_cells
    views = shear_rate.shape[0]
    padded_width = width + 2 * rim_width
    rows_in = jnp.arange(padded_width, dtype=jnp.int32)[None, :, None]
    cols_out = jnp.arange(width, dtype=jnp.int32)[None, None, :]

    def march(state_pair, local_depth):
        colour, through = state_pair
        depth_index = slab_first + local_depth
        offset = shear_rate * (depth_index.astype(jnp.float32) + 0.5 - 0.5 * depth_total)
        floor_part = jnp.floor(offset)
        fraction = offset - floor_part
        start = floor_part.astype(jnp.int32) + rim_width
        target = cols_out + start[:, None, None]
        resample = jnp.where(rows_in == target, (1.0 - fraction)[:, None, None], 0.0) + jnp.where(
            rows_in == target + 1, fraction[:, None, None], 0.0
        )
        depth_plane = lax.dynamic_index_in_dim(rimmed, local_depth, 1, keepdims=False)
        samples = jnp.einsum(
            "fyp,vpx->vfyx", depth_plane, resample, precision=lax.Precision.HIGHEST
        )
        logits = (
            colour_weight[:, None, :, 0, None] * samples[:, 0][:, :, None, :]
            + colour_weight[:, None, :, 1, None] * samples[:, 1][:, :, None, :]
            + colour_bias[:, None, :, None]
        )
        colours = jax.nn.sigmoid(logits[:, :, :3, :])
        fading = jnp.exp(-RAY_STEP * jax.nn.softplus(logits[:, :, 3, :]))
        colour = colour + (through * (1.0 - fading))[:, :, None, :] * colours
        return ((colour, through * fading), None)

    start_state = (
        jnp.zeros((views, rows, 3, width), jnp.float32),
        jnp.ones((views, rows, width), jnp.float32),
    )
    (colour, through), unused = lax.scan(
        march, start_state, jnp.arange(depth_cells, dtype=jnp.int32)
    )
    slab = jnp.concatenate([colour, (1.0 - through)[:, :, None, :]], axis=2)
    view_count = views // depth_devices
    view_first = lax.axis_index("depth") * view_count
    everything = lax.all_gather(slab[None], "depth", axis=0, tiled=True)
    stack = lax.dynamic_slice_in_dim(everything, view_first, view_count, 1)
    own_order = lax.dynamic_slice_in_dim(slab_order, view_first, view_count, 0)
    slab_ids = jnp.arange(depth_devices, dtype=jnp.int32)

    def pick(position):
        chooser = (own_order[:, position][None, :] == slab_ids[:, None]).astype(jnp.float32)
        return jnp.sum(chooser[:, :, None, None, None] * stack, axis=0)

    result = pick(0)
    for position in range(1, depth_devices):
        result = result + (1.0 - result[:, :, 3:4, :]) * pick(position)
    picture = result.astype(jnp.bfloat16)
    column = jnp.arange(width, dtype=jnp.int32)
    keep = column[None, None, :] < lengths[:, 0, :, None]
    pieces = jnp.where(keep[:, :, None, :], picture, jnp.zeros((), jnp.bfloat16))
    tiles = lax.axis_size("col")
    capacity = 2 * rows // tiles
    mine = owners[:, 0, :, 0]
    slot_rank = slot_plan(mine, tiles)
    tile_ids = jnp.arange(tiles, dtype=jnp.int32)
    slot_ids = jnp.arange(capacity, dtype=jnp.int32)
    select = (mine[:, None, None, :] == tile_ids[None, :, None, None]) & (
        slot_rank[:, None, None, :] == slot_ids[None, None, :, None]
    )
    outgoing = jnp.einsum(
        "vosy,vycx->voscx", select.astype(jnp.bfloat16), pieces, preferred_element_type=jnp.float32
    ).astype(jnp.bfloat16)
    incoming = lax.all_to_all(outgoing, "col", split_axis=1, concat_axis=1, tiled=True)
    this_tile = lax.axis_index("col")
    owner_map = lax.all_gather(owners, "col", axis=1, tiled=True)[:, :, :, 0]
    source_rank = slot_plan(owner_map, tiles)
    place = (owner_map[:, :, None, :] == this_tile) & (
        source_rank[:, :, None, :] == slot_ids[None, None, :, None]
    )
    warp_own = lax.dynamic_slice_in_dim(warp_matrix, view_first, view_count, 0)
    warped = jnp.einsum("vtscx,vxz->vtscz", incoming, warp_own, preferred_element_type=jnp.float32)
    frame = jnp.einsum(
        "vtsy,vtscz->vycz", place.astype(jnp.float32), warped, precision=lax.Precision.HIGHEST
    )
    return (species_out, frame)


def solution(mesh):
    in_specs = (
        P(None, "depth", "row", "col"),
        P("depth", "row", "col"),
        P("depth", "row", "col"),
        P(),
        P(),
        P(),
        P(),
        P("depth", "col", "row"),
        P("depth", "col", "row", None),
        P(),
    )
    out_specs = (P(None, "depth", "row", "col"), P("depth", "row", None, "col"))
    return jax.shard_map(body, mesh=mesh, in_specs=in_specs, out_specs=out_specs, check_vma=False)
```

profile of v0, /device:TPU:0, one launch (start us, length us, event | category | flops | bytes accessed | tf_op | source)
XLA Modules:
  0.0 256.1 jit_solution(864567025671548358)
XLA Ops:
  7.2 1.3 pad_maximum_fusion.2
  9.4 5.6 %collective-permute-start = (f32[4,16,32,6]{2,1,3,0:T(8,128)S(1)}, f32[4,16,32,6]{2,1,3,0:T(8,128)}, u32[]{:S(2)}, u32[]{:S(2)}) collective-permute-start(f32[4,16,32,6]{2,1,3,0:T(8,128)S(1)} %copy.101), channel_id=1, source_target_pairs={{0,1},{1,2},{2,3},{4,5},{5,6},{6,7},{8,9},{9,10},{10,11},{12,13},{... | collective-permute-start | bytes 147464 | tf_op jit(solution)/shard_map/ppermute | solution.py:21
  15.1 1.1 copy.102
  16.2 1.3 collective-permute-start.1
  17.6 0.9 collective-permute-done
  18.5 1.4 copy.81
  19.9 4.9 %collective-permute-done.1 = f32[4,16,32,6]{2,1,3,0:T(8,128)} collective-permute-done((f32[4,16,32,6]{2,1,3,0:T(8,128)}, f32[4,16,32,6]{2,1,3,0:T(8,128)}, u32[]{:S(2)}, u32[]{:S(2)}) %collective-permute-start.1) | collective-permute-done | bytes 49184 | tf_op jit(solution)/shard_map/ppermute | solution.py:23
  24.8 1.4 copy.82
  26.2 2.3 pad_maximum_fusion.5
  28.4 4.1 %collective-permute-start.2 = (f32[4,3,32,140]{3,2,1,0:T(8,128)}, f32[4,3,32,140]{3,2,1,0:T(8,128)}, u32[]{:S(2)}, u32[]{:S(2)}) collective-permute-start(f32[4,3,32,140]{3,2,1,0:T(8,128)} %get-tuple-element.427), channel_id=1, source_target_pairs={{0,8},{8,16},{16,24},{1,9},{9,17},{17,25},{2,10},{10,18},{18,26},{... | collective-permute-start | bytes 645128 | tf_op jit(solution)/shard_map/ppermute | solution.py:21
  32.6 1.3 collective-permute-start.3
  34.1 1.0 slice.313
  35.1 1.0 slice.311
  36.4 2.9 %collective-permute-done.2 = f32[4,3,32,140]{3,2,1,0:T(8,128)} collective-permute-done((f32[4,3,32,140]{3,2,1,0:T(8,128)}, f32[4,3,32,140]{3,2,1,0:T(8,128)}, u32[]{:S(2)}, u32[]{:S(2)}) %collective-permute-start.2) | collective-permute-done | bytes 215072 | tf_op jit(solution)/shard_map/ppermute | solution.py:21
  39.3 10.4 %collective-permute-done.3 = f32[4,3,32,140]{3,2,1,0:T(8,128)} collective-permute-done((f32[4,3,32,140]{3,2,1,0:T(8,128)}, f32[4,3,32,140]{3,2,1,0:T(8,128)}, u32[]{:S(2)}, u32[]{:S(2)}) %collective-permute-start.3) | collective-permute-done | bytes 215072 | tf_op jit(solution)/shard_map/ppermute | solution.py:23
  49.7 1.7 pad_maximum_fusion.12
  51.6 1.4 collective-permute-start.4
  53.1 1.5 collective-permute-start.5
  54.6 0.9 pad_maximum_fusion.1
  55.6 0.9 collective-permute-done.5
  56.7 4.4 %pad_maximum_fusion = f32[4,22,38,140]{3,2,1,0:T(8,128)S(1)} fusion(f32[4,22,3,140]{3,2,1,0:T(4,128)S(1)} %copy.86, f32[4,3,32,140]{3,2,1,0:T(8,128)} %collective-permute-done.3, f32[4,16,32,6]{3,2,1,0:T(8,128)S(1)} %copy-done.2, f32[1,16,32,128]{3,2,1,0:T(8,128)S(1)} %bitcast.145, f32[1,16,32,128]{3,2,1,0:T(8,128)S(1)} %bitcast.150, ...), kind=kLoop, calls=%fused_computation.42 | loop fusion | flops 3745280 | bytes 3745280 | tf_op jit(solution)/shard_map/concatenate | solution.py:19
  62.0 0.8 negate_bitcast_fusion
  62.9 2.9 %fusion.31 = f32[2,20,36,138]{3,2,1,0:T(8,128)S(1)} fusion(f32[4,22,38,140]{3,2,1,0:T(8,128)S(1)} %pad_maximum_fusion, f32[1,20,36,138]{3,2,1,0:T(8,128)S(1)} %bitcast.151, f32[1,20,36,138]{3,2,1,0:T(8,128)S(1)} %get-tuple-element.413, f32[20,36,138]{2,1,0:T(8,128)S(1)} %slice.316, pred[20,36,138]{2,1,0:T(8,128)(4,1)S(1)} %copy-done.9), kind=kLoop, calls=%fused_computation.51 | loop fusion | flops 4371840 | bytes 7650720 | tf_op jit(solution)/shard_map/jit(_where)/select_n | solution.py:88
  66.8 3.0 %fusion.42 = f32[2,18,34,136]{3,2,1,0:T(8,128)S(1)} fusion(f32[2,20,36,138]{3,2,1,0:T(8,128)S(1)} %fusion.31, f32[4,22,38,140]{3,2,1,0:T(8,128)S(1)} %pad_maximum_fusion, f32[1,18,34,136]{3,2,1,0:T(8,128)S(1)} %bitcast.152, f32[1,18,34,136]{3,2,1,0:T(8,128)S(1)} %get-tuple-element.411, f32[18,34,136]{2,1,0:T(8,128)S(1)} %slice.328, ...), kind=kLoop, calls=%fused_computation.65 | loop fusion | flops 4161600 | bytes 7074720 | tf_op jit(solution)/shard_map/jit(_where)/select_n | solution.py:92
  70.4 2.0 fusion.53
  72.4 106.2 %while.18 = (s32[]{:T(128)}, f32[16,32,3,128]{3,2,1,0:T(4,128)S(1)}, f32[16,32,128]{2,1,0:T(8,128)S(1)}, f32[16,4,2]{0,1,2:T(4,128)S(1)}, s32[16]{0:T(128)S(1)},...) while((s32[]{:T(128)}, ...), condition=%wide.region_5.6_spmd.clone.clone, body=%wide.region_4.5_spmd.clone.clone.sunk | while | flops 215089280 | bytes 12881818 | solution.py:161
  72.6 0.7 dynamic_slice.52
  76.0 1.2 convolution_bitcast_fusion.3
  79.2 0.7 dynamic_slice.52
  82.6 1.2 convolution_bitcast_fusion.3
  85.9 0.7 dynamic_slice.52
  89.2 1.2 convolution_bitcast_fusion.3
  92.5 0.7 dynamic_slice.52
  95.9 1.2 convolution_bitcast_fusion.3
  99.1 0.7 dynamic_slice.52
  102.5 1.2 convolution_bitcast_fusion.3
  105.7 0.7 dynamic_slice.52
  109.1 1.2 convolution_bitcast_fusion.3
  112.4 0.7 dynamic_slice.52
  115.7 1.2 convolution_bitcast_fusion.3
  119.0 0.7 dynamic_slice.52
  122.3 1.2 convolution_bitcast_fusion.3
  125.6 0.7 dynamic_slice.52
  129.0 1.2 convolution_bitcast_fusion.3
  132.2 0.7 dynamic_slice.52
  135.6 1.2 convolution_bitcast_fusion.3
  138.8 0.7 dynamic_slice.52
  142.2 1.2 convolution_bitcast_fusion.3
  145.5 0.7 dynamic_slice.52
  148.8 1.2 convolution_bitcast_fusion.3
  155.4 1.2 convolution_bitcast_fusion.3
  162.1 1.2 convolution_bitcast_fusion.3
  165.3 0.7 dynamic_slice.52
  168.7 1.2 convolution_bitcast_fusion.3
  175.3 1.2 convolution_bitcast_fusion.3
  178.7 1.1 pad_maximum_fusion.3
  180.0 8.5 %all_gather.6 = s32[4,4,32,1]{2,3,1,0:T(1,128)S(1)} all-gather(s32[4,1,32,1]{2,3,1,0:T(1,128)S(1)} %copy-done.11), channel_id=1, replica_groups=mesh['depth'=4,'row'=2,'col'=4] {'col'}, dimensions={1}, use_global_device_ids=true | all-gather | bytes 2560 | tf_op jit(solution)/shard_map/all_gather | solution.py:197
  189.1 42.2 %all-gather.3.cloned.1.call-done = f32[64,32,4,128]{3,1,2,0:T(8,128)} async-done(((f32[16,32,4,128]{3,1,2,0:T(8,128)}), f32[64,32,4,128]{3,1,2,0:T(8,128)}) %all-gather.3.cloned.1.call-update) | async-done | bytes 4194320 | tf_op jit(solution)/shard_map/all_gather | solution.py:167
  231.3 1.7 multiply_reduce_fusion
  233.5 0.8 copy.91
  234.3 4.6 %all-to-all-start = ((bf16[4,4,16,4,128]{4,3,2,0,1:T(4,128)(2,1)}), bf16[4,4,16,4,128]{4,3,2,0,1:T(4,128)(2,1)S(1)}, u32[]{:S(2)}, u32[]{:S(2)}) async-start(bf16[4,4,16,4,128]{4,3,2,0,1:T(4,128)(2,1)} %copy.91), calls=%async_computation | async-start | bytes 524288 | tf_op jit(solution)/shard_map/all_to_all | solution.py:195
  239.6 1.0 slice.349
  240.6 7.2 %all-to-all-done = bf16[4,4,16,4,128]{4,3,2,0,1:T(4,128)(2,1)S(1)} async-done(((bf16[4,4,16,4,128]{4,3,2,0,1:T(4,128)(2,1)}), bf16[4,4,16,4,128]{4,3,2,0,1:T(4,128)(2,1)S(1)}, u32[]{:S(2)}, u32[]{:S(2)}) %all-to-all-start) | async-done | bytes 262176 | tf_op jit(solution)/shard_map/all_to_all | solution.py:195
  248.4 0.9 copy.93
  (309 shorter events, 42.9 us)
Async XLA Ops:
  7.2 240.6 %copy-start = (bf16[16,128,128]{2,1,0:T(8,128)(2,1)S(1)}, bf16[16,128,128]{2,1,0:T(8,128)(2,1)}, u32[]{:S(2)}) copy-start(bf16[16,128,128]{2,1,0:T(8,128)(2,1)} %param.21) | copy-start | bytes 1572868
  7.2 224.1 %all-gather.3.cloned.1.call-start = ((), (), s32[]{:S(2)}) async-start(), calls=%async_computation.1 | async-start | bytes 5242880 | tf_op jit(solution)/shard_map/all_gather | solution.py:167
  9.4 9.1 %collective-permute-start = (f32[4,16,32,6]{2,1,3,0:T(8,128)S(1)}, f32[4,16,32,6]{2,1,3,0:T(8,128)}, u32[]{:S(2)}, u32[]{:S(2)}) collective-permute-start(f32[4,16,32,6]{2,1,3,0:T(8,128)S(1)} %copy.101), channel_id=1, source_target_pairs={{0,1},{1,2},{2,3},{4,5},{5,6},{6,7},{8,9},{9,10},{10,11},{12,13},{... | collective-permute-start | bytes 147464 | tf_op jit(solution)/shard_map/ppermute | solution.py:21
  15.1 11.1 %copy-start.3 = (f32[2,16,32,128]{3,2,1,0:T(8,128)S(1)}, f32[2,16,32,128]{3,2,1,0:T(8,128)}, u32[]{:S(2)}) copy-start(f32[2,16,32,128]{3,2,1,0:T(8,128)} %param.12) | copy-start | bytes 1572868
  15.1 11.1 %copy-start.4 = (f32[16,32,128]{2,1,0:T(8,128)S(1)}, f32[16,32,128]{2,1,0:T(8,128)}, u32[]{:S(2)}) copy-start(f32[16,32,128]{2,1,0:T(8,128)} %param.14) | copy-start | bytes 786436
  16.2 8.6 %collective-permute-start.1 = (f32[4,16,32,6]{2,1,3,0:T(8,128)}, f32[4,16,32,6]{2,1,3,0:T(8,128)}, u32[]{:S(2)}, u32[]{:S(2)}) collective-permute-start(f32[4,16,32,6]{2,1,3,0:T(8,128)} %copy.102), channel_id=1, source_target_pairs={{1,0},{2,1},{3,2},{5,4},{6,5},{7,6},{9,8},{10,9},{11,10},{13,12},{... | collective-permute-start | bytes 147464 | tf_op jit(solution)/shard_map/ppermute | solution.py:23
  26.2 2.3 copy-start.1
  26.2 10.1 %copy-start.14 = (f32[16,4]{0,1:T(4,128)S(1)}, f32[16,4]{0,1:T(4,128)}, u32[]{:S(2)}) copy-start(f32[16,4]{0,1:T(4,128)} %param.17) | copy-start | bytes 772
  26.2 10.2 %copy-start.13 = (f32[16,4,2]{0,2,1:T(2,128)S(1)}, f32[16,4,2]{0,2,1:T(2,128)}, u32[]{:S(2)}) copy-start(f32[16,4,2]{0,2,1:T(2,128)} %param.16) | copy-start | bytes 1540
  28.4 10.9 %collective-permute-start.2 = (f32[4,3,32,140]{3,2,1,0:T(8,128)}, f32[4,3,32,140]{3,2,1,0:T(8,128)}, u32[]{:S(2)}, u32[]{:S(2)}) collective-permute-start(f32[4,3,32,140]{3,2,1,0:T(8,128)} %get-tuple-element.427), channel_id=1, source_target_pairs={{0,8},{8,16},{16,24},{1,9},{9,17},{17,25},{2,10},{10,18},{18,26},{... | collective-permute-start | bytes 645128 | tf_op jit(solution)/shard_map/ppermute | solution.py:21
  32.6 17.1 %collective-permute-start.3 = (f32[4,3,32,140]{3,2,1,0:T(8,128)}, f32[4,3,32,140]{3,2,1,0:T(8,128)}, u32[]{:S(2)}, u32[]{:S(2)}) collective-permute-start(f32[4,3,32,140]{3,2,1,0:T(8,128)} %get-tuple-element.428), channel_id=1, source_target_pairs={{8,0},{16,8},{24,16},{9,1},{17,9},{25,17},{10,2},{18,10},{26,18},{... | collective-permute-start | bytes 645128 | tf_op jit(solution)/shard_map/ppermute | solution.py:23
  36.4 18.2 %copy-start.5 = (f32[16,32,128]{2,1,0:T(8,128)S(1)}, f32[16,32,128]{2,1,0:T(8,128)}, u32[]{:S(2)}) copy-start(f32[16,32,128]{2,1,0:T(8,128)} %param.14) | copy-start | bytes 786436
  36.4 18.2 %copy-start.6 = (f32[16,32,128]{2,1,0:T(8,128)S(1)}, f32[16,32,128]{2,1,0:T(8,128)}, u32[]{:S(2)}) copy-start(f32[16,32,128]{2,1,0:T(8,128)} %param.13) | copy-start | bytes 786436
  51.4 3.2 %copy-start.2 = (f32[4,16,32,6]{3,2,1,0:T(8,128)S(1)}, f32[4,16,32,6]{3,2,1,0:T(8,128)}, u32[]{:S(2)}) copy-start(f32[4,16,32,6]{3,2,1,0:T(8,128)} %copy-done.1) | copy-start | bytes 147460
  51.6 4.0 %collective-permute-start.4 = (f32[4,22,3,140]{3,0,2,1:T(4,128)S(1)}, f32[4,22,3,140]{3,0,2,1:T(4,128)S(1)}, u32[]{:S(2)}, u32[]{:S(2)}) collective-permute-start(f32[4,22,3,140]{3,0,2,1:T(4,128)S(1)} %copy.103), channel_id=1, source_target_pairs={{0,4},{1,5},{2,6},{3,7},{8,12},{9,13},{10,14},{11,15},{16,20},{17,... | collective-permute-start | bytes 443528 | tf_op jit(solution)/shard_map/ppermute | solution.py:21
  53.1 3.4 %collective-permute-start.5 = (f32[4,22,3,140]{3,0,2,1:T(4,128)S(1)}, f32[4,22,3,140]{3,0,2,1:T(4,128)S(1)}, u32[]{:S(2)}, u32[]{:S(2)}) collective-permute-start(f32[4,22,3,140]{3,0,2,1:T(4,128)S(1)} %copy.104), channel_id=1, source_target_pairs={{4,0},{5,1},{6,2},{7,3},{12,8},{13,9},{14,10},{15,11},{20,16},{21,... | collective-permute-start | bytes 443528 | tf_op jit(solution)/shard_map/ppermute | solution.py:23
  62.0 0.9 copy-start.9
  65.9 0.9 copy-start.10
  70.4 2.0 copy-start.12
  72.6 3.4 %copy-start.7 = (f32[2,16,32,134]{3,2,1,0:T(8,128)}, f32[2,16,32,134]{3,2,1,0:T(8,128)S(1)}, u32[]{:S(2)}) copy-start(f32[2,16,32,134]{3,2,1,0:T(8,128)S(1)} %get-tuple-element.547) | copy-start | bytes 1646596 | tf_op jit(solution)/shard_map/while
  78.0 1.2 copy-start.8
  79.2 3.4 %copy-start.7 = (f32[2,16,32,134]{3,2,1,0:T(8,128)}, f32[2,16,32,134]{3,2,1,0:T(8,128)S(1)}, u32[]{:S(2)}) copy-start(f32[2,16,32,134]{3,2,1,0:T(8,128)S(1)} %get-tuple-element.547) | copy-start | bytes 1646596 | tf_op jit(solution)/shard_map/while
  84.6 1.2 copy-start.8
  85.9 3.4 %copy-start.7 = (f32[2,16,32,134]{3,2,1,0:T(8,128)}, f32[2,16,32,134]{3,2,1,0:T(8,128)S(1)}, u32[]{:S(2)}) copy-start(f32[2,16,32,134]{3,2,1,0:T(8,128)S(1)} %get-tuple-element.547) | copy-start | bytes 1646596 | tf_op jit(solution)/shard_map/while
  91.3 1.2 copy-start.8
  92.5 3.4 %copy-start.7 = (f32[2,16,32,134]{3,2,1,0:T(8,128)}, f32[2,16,32,134]{3,2,1,0:T(8,128)S(1)}, u32[]{:S(2)}) copy-start(f32[2,16,32,134]{3,2,1,0:T(8,128)S(1)} %get-tuple-element.547) | copy-start | bytes 1646596 | tf_op jit(solution)/shard_map/while
  97.9 1.2 copy-start.8
  99.1 3.4 %copy-start.7 = (f32[2,16,32,134]{3,2,1,0:T(8,128)}, f32[2,16,32,134]{3,2,1,0:T(8,128)S(1)}, u32[]{:S(2)}) copy-start(f32[2,16,32,134]{3,2,1,0:T(8,128)S(1)} %get-tuple-element.547) | copy-start | bytes 1646596 | tf_op jit(solution)/shard_map/while
  104.5 1.2 copy-start.8
  105.7 3.4 %copy-start.7 = (f32[2,16,32,134]{3,2,1,0:T(8,128)}, f32[2,16,32,134]{3,2,1,0:T(8,128)S(1)}, u32[]{:S(2)}) copy-start(f32[2,16,32,134]{3,2,1,0:T(8,128)S(1)} %get-tuple-element.547) | copy-start | bytes 1646596 | tf_op jit(solution)/shard_map/while
  111.1 1.2 copy-start.8
  112.4 3.4 %copy-start.7 = (f32[2,16,32,134]{3,2,1,0:T(8,128)}, f32[2,16,32,134]{3,2,1,0:T(8,128)S(1)}, u32[]{:S(2)}) copy-start(f32[2,16,32,134]{3,2,1,0:T(8,128)S(1)} %get-tuple-element.547) | copy-start | bytes 1646596 | tf_op jit(solution)/shard_map/while
  117.8 1.2 copy-start.8
  119.0 3.4 %copy-start.7 = (f32[2,16,32,134]{3,2,1,0:T(8,128)}, f32[2,16,32,134]{3,2,1,0:T(8,128)S(1)}, u32[]{:S(2)}) copy-start(f32[2,16,32,134]{3,2,1,0:T(8,128)S(1)} %get-tuple-element.547) | copy-start | bytes 1646596 | tf_op jit(solution)/shard_map/while
  124.4 1.2 copy-start.8
  125.6 3.4 %copy-start.7 = (f32[2,16,32,134]{3,2,1,0:T(8,128)}, f32[2,16,32,134]{3,2,1,0:T(8,128)S(1)}, u32[]{:S(2)}) copy-start(f32[2,16,32,134]{3,2,1,0:T(8,128)S(1)} %get-tuple-element.547) | copy-start | bytes 1646596 | tf_op jit(solution)/shard_map/while
  131.0 1.2 copy-start.8
  132.2 3.4 %copy-start.7 = (f32[2,16,32,134]{3,2,1,0:T(8,128)}, f32[2,16,32,134]{3,2,1,0:T(8,128)S(1)}, u32[]{:S(2)}) copy-start(f32[2,16,32,134]{3,2,1,0:T(8,128)S(1)} %get-tuple-element.547) | copy-start | bytes 1646596 | tf_op jit(solution)/shard_map/while
  137.6 1.2 copy-start.8
  138.8 3.4 %copy-start.7 = (f32[2,16,32,134]{3,2,1,0:T(8,128)}, f32[2,16,32,134]{3,2,1,0:T(8,128)S(1)}, u32[]{:S(2)}) copy-start(f32[2,16,32,134]{3,2,1,0:T(8,128)S(1)} %get-tuple-element.547) | copy-start | bytes 1646596 | tf_op jit(solution)/shard_map/while
  144.2 1.2 copy-start.8
  145.5 3.4 %copy-start.7 = (f32[2,16,32,134]{3,2,1,0:T(8,128)}, f32[2,16,32,134]{3,2,1,0:T(8,128)S(1)}, u32[]{:S(2)}) copy-start(f32[2,16,32,134]{3,2,1,0:T(8,128)S(1)} %get-tuple-element.547) | copy-start | bytes 1646596 | tf_op jit(solution)/shard_map/while
  150.9 1.2 copy-start.8
  152.1 3.4 %copy-start.7 = (f32[2,16,32,134]{3,2,1,0:T(8,128)}, f32[2,16,32,134]{3,2,1,0:T(8,128)S(1)}, u32[]{:S(2)}) copy-start(f32[2,16,32,134]{3,2,1,0:T(8,128)S(1)} %get-tuple-element.547) | copy-start | bytes 1646596 | tf_op jit(solution)/shard_map/while
  157.5 1.2 copy-start.8
  158.7 3.4 %copy-start.7 = (f32[2,16,32,134]{3,2,1,0:T(8,128)}, f32[2,16,32,134]{3,2,1,0:T(8,128)S(1)}, u32[]{:S(2)}) copy-start(f32[2,16,32,134]{3,2,1,0:T(8,128)S(1)} %get-tuple-element.547) | copy-start | bytes 1646596 | tf_op jit(solution)/shard_map/while
  164.1 1.2 copy-start.8
  165.3 3.4 %copy-start.7 = (f32[2,16,32,134]{3,2,1,0:T(8,128)}, f32[2,16,32,134]{3,2,1,0:T(8,128)S(1)}, u32[]{:S(2)}) copy-start(f32[2,16,32,134]{3,2,1,0:T(8,128)S(1)} %get-tuple-element.547) | copy-start | bytes 1646596 | tf_op jit(solution)/shard_map/while
  170.7 1.2 copy-start.8
  172.0 3.4 %copy-start.7 = (f32[2,16,32,134]{3,2,1,0:T(8,128)}, f32[2,16,32,134]{3,2,1,0:T(8,128)S(1)}, u32[]{:S(2)}) copy-start(f32[2,16,32,134]{3,2,1,0:T(8,128)S(1)} %get-tuple-element.547) | copy-start | bytes 1646596 | tf_op jit(solution)/shard_map/while
  177.3 1.2 copy-start.8
  178.7 1.1 copy-start.11
  178.7 9.8 %copy-start.16 = (s32[16,4]{0,1:T(4,128)S(1)}, s32[16,4]{0,1:T(4,128)}, u32[]{:S(2)}) copy-start(s32[16,4]{0,1:T(4,128)} %param.18) | copy-start | bytes 772
  178.7 10.2 %copy-start.15 = (s32[4,1,32]{2,1,0:T(1,128)S(1)}, s32[4,1,32]{2,1,0:T(1,128)}, u32[]{:S(2)}) copy-start(s32[4,1,32]{2,1,0:T(1,128)} %param.19) | copy-start | bytes 1540
  234.3 13.5 %all-to-all-start = ((bf16[4,4,16,4,128]{4,3,2,0,1:T(4,128)(2,1)}), bf16[4,4,16,4,128]{4,3,2,0,1:T(4,128)(2,1)S(1)}, u32[]{:S(2)}, u32[]{:S(2)}) async-start(bf16[4,4,16,4,128]{4,3,2,0,1:T(4,128)(2,1)} %copy.91), calls=%async_computation | async-start | bytes 524288 | tf_op jit(solution)/shard_map/all_to_all | solution.py:195
Sparse Core Ops, SparseCore 0:
  179.9 51.3 all-gather.2
where the time goes:
time: 258 us; the launch traced here: 256 us
  waiting for transfers between devices  69.4 us (27%)
  local copies, waits for them, and re-layouts  43.7 us (17%)
  loops' own time  43 us (17%)
  other arithmetic  37.8 us (15%)
  starting transfers between devices  19.9 us (8%)
  matrix products  19.3 us (7%)
  between operations  14.6 us (6%)
  blocking collectives  8.53 us (3%)
    another operation x1, loops' own time, body(): lax.scan(march, start_state, jnp.arange(depth_cells, dtype=jnp.int32))  43 us
    all_gather x1, waiting for transfers between devices, body(): everything = lax.all_gather(slab[None], 'depth', axis=0, tiled=True)  42.2 us
    while x96, local copies, waits for them, and re-layouts  20.6 us
    dot_general x16, matrix products, march(): jnp.einsum('fyp,vpx->vfyx', depth_plane, resample, precision=lax.Precisio...  18.5 us
    ppermute x3, waiting for transfers between devices, with_halo(): lax.ppermute(head, axis, [((i + 1) % count, i) for i in range(ends)])  16.2 us
    ppermute x3, starting transfers between devices, with_halo(): lax.ppermute(tail, axis, [(i, (i + 1) % count) for i in range(ends)])  11.2 us
    dynamic_slice x16, local copies, waits for them, and re-layouts, body(): lax.scan(march, start_state, jnp.arange(depth_cells, dtype=jnp.int32))  10.7 us
    all_gather x1, blocking collectives, body(): owner_map = lax.all_gather(owners, 'col', axis=1, tiled=True)[:, :, :, 0]  8.53 us
  transfers between devices with their start and end apart: 8, of which 7 were waited for; matrix products, arithmetic and copies ran while one was open for 3% of the time, Pallas kernels for 0%

commit v1 on v0

v1 whole, which is shorter than its diff:
```python
import functools

import jax
import jax.numpy as jnp
from jax import lax
from jax.experimental import pallas as pl
from jax.experimental.pallas import tpu as pltpu
from jax.sharding import PartitionSpec as P

TIME_STEP = 0.1
RAY_STEP = 0.02
VEL_DEPTH = 0.3
VEL_ROW = 0.2
VEL_COL = 0.4


def with_halo(cells, sides, width):
    for axis, dim in sides:
        count = lax.axis_size(axis)
        ends = count - 1
        head = lax.slice_in_dim(cells, 0, width, axis=dim)
        tail = lax.slice_in_dim(cells, cells.shape[dim] - width, cells.shape[dim], axis=dim)
        cells = jnp.concatenate(
            [
                lax.ppermute(tail, axis, [(i, (i + 1) % count) for i in range(ends)]),
                cells,
                lax.ppermute(head, axis, [((i + 1) % count, i) for i in range(ends)]),
            ],
            axis=dim,
        )
    return cells


def tendency_of(padded, diffusivity, reaction_rate):
    centre = padded[:, 1:-1, 1:-1, 1:-1]
    below_depth = padded[:, :-2, 1:-1, 1:-1]
    above_depth = padded[:, 2:, 1:-1, 1:-1]
    below_row = padded[:, 1:-1, :-2, 1:-1]
    above_row = padded[:, 1:-1, 2:, 1:-1]
    below_col = padded[:, 1:-1, 1:-1, :-2]
    above_col = padded[:, 1:-1, 1:-1, 2:]
    laplace = (
        below_depth + above_depth + below_row + above_row + below_col + above_col - 6.0 * centre
    )
    advect = (
        VEL_DEPTH * (centre - below_depth)
        + VEL_ROW * (centre - below_row)
        + VEL_COL * (centre - below_col)
    )
    heat_part = centre[1]
    burned = reaction_rate * centre[0] * heat_part * heat_part / (1.0 + heat_part * heat_part)
    source = jnp.stack([-burned, burned])
    return diffusivity * laplace - advect + source


def trimmed(array, layers):
    depth_len = array.shape[-3]
    row_len = array.shape[-2]
    col_len = array.shape[-1]
    return array[
        ..., layers : depth_len - layers, layers : row_len - layers, layers : col_len - layers
    ]


def inside_grid(first_index, count, margin, total):
    places = first_index - margin + jnp.arange(count + 2 * margin, dtype=jnp.int32)
    return (places >= 0) & (places < total)


def advance_deep(species, diffusivity, reaction_rate, rim_width):
    depth_cells = species.shape[1]
    rows = species.shape[2]
    width = species.shape[3]
    packed = jnp.concatenate([species, diffusivity[None], reaction_rate[None]], axis=0)
    wide = with_halo(packed, (("col", 3),), 3 + rim_width)
    deep = with_halo(wide, (("depth", 1), ("row", 2)), 3)
    depth_ok = inside_grid(
        lax.axis_index("depth") * depth_cells, depth_cells, 3, depth_cells * lax.axis_size("depth")
    )
    row_ok = inside_grid(lax.axis_index("row") * rows, rows, 3, rows * lax.axis_size("row"))
    col_ok = inside_grid(
        lax.axis_index("col") * width, width, 3 + rim_width, width * lax.axis_size("col")
    )
    inside = depth_ok[:, None, None] & row_ok[None, :, None] & col_ok[None, None, :]
    fields = deep[:2]
    spread = deep[2]
    rates = deep[3]
    zero = jnp.zeros((), jnp.float32)
    first = trimmed(fields, 1) + TIME_STEP * tendency_of(
        fields, trimmed(spread, 1), trimmed(rates, 1)
    )
    first = jnp.where(trimmed(inside, 1)[None], first, zero)
    second = 0.75 * trimmed(fields, 2) + 0.25 * (
        trimmed(first, 1) + TIME_STEP * tendency_of(first, trimmed(spread, 2), trimmed(rates, 2))
    )
    second = jnp.where(trimmed(inside, 2)[None], second, zero)
    final = trimmed(fields, 3) / 3.0 + 2.0 / 3.0 * (
        trimmed(second, 1) + TIME_STEP * tendency_of(second, trimmed(spread, 3), trimmed(rates, 3))
    )
    final = jnp.where(trimmed(inside, 3)[None], final, zero)
    return final


MESH = pl.DeviceIdType.MESH


def march_kernel(
    depth_devices, tiles, capacity,
    start_ref, fraction_ref, weight_ref, bias_ref, order_ref,
    rimmed_ref, length_ref, key_by_channel_ref, key_by_row_ref, warp_ref,
    frame_ref,
    shifted, *scratch,
):
    view_count = frame_ref.shape[0]
    stacks = scratch[:view_count]
    images = scratch[view_count : 2 * view_count]
    packs = scratch[2 * view_count : 3 * view_count]
    arrivals = scratch[3 * view_count : 4 * view_count]
    keys, slab_send, slab_recv, tile_send, tile_recv, key_send, key_recv = scratch[4 * view_count :]
    depth_cells, rows, width = shifted.shape[0], shifted.shape[3], shifted.shape[4]
    shifts = shifted.shape[1]
    me_d, me_r, me_c = lax.axis_index("depth"), lax.axis_index("row"), lax.axis_index("col")

    def slab_of(step):
        return lax.rem(me_d + step, depth_devices)

    def tile_of(step):
        return lax.rem(me_c + step, tiles)

    barrier = pltpu.get_barrier_semaphore()
    for step in range(1, depth_devices):
        pl.semaphore_signal(barrier, inc=1, device_id=(slab_of(step), me_r, me_c), device_id_type=MESH)
    for step in range(1, tiles):
        pl.semaphore_signal(barrier, inc=1, device_id=(me_d, me_r, tile_of(step)), device_id_type=MESH)

    def shift_planes(cell, carry):
        for field in range(2):
            plane = rimmed_ref[field, cell]
            for shift in range(shifts):
                here = plane[:, shift : shift + width]
                shifted[cell, shift, 2 * field] = here
                shifted[cell, shift, 2 * field + 1] = plane[:, shift + 1 : shift + 1 + width] - here
        return carry

    lax.fori_loop(0, depth_cells, shift_planes, 0)
    pl.semaphore_wait(barrier, depth_devices - 1 + tiles - 1)

    key_copies = []
    for step in range(1, tiles):
        copy = pltpu.make_async_remote_copy(
            src_ref=key_by_row_ref, dst_ref=keys.at[me_c],
            send_sem=key_send.at[step], recv_sem=key_recv.at[step],
            device_id=(me_d, me_r, tile_of(step)), device_id_type=MESH,
        )
        copy.start()
        key_copies.append(copy)
    keys[me_c] = key_by_row_ref[...]

    def render(view, out_ref):
        weights = [[weight_ref[view, c, f] for f in range(2)] for c in range(4)]
        biases = [bias_ref[view, c] for c in range(4)]

        def cells(cell, state):
            red, green, blue, through = state
            at = start_ref[view, cell]
            fraction = fraction_ref[view, cell]
            s0 = shifted[cell, at, 0] + fraction * shifted[cell, at, 1]
            s1 = shifted[cell, at, 2] + fraction * shifted[cell, at, 3]
            logits = [weights[c][0] * s0 + weights[c][1] * s1 + biases[c] for c in range(4)]
            fading = jnp.exp(-RAY_STEP * jnp.log(1.0 + jnp.exp(logits[3])))
            later = through * fading
            share = through - later
            return (
                red + share * jnp.tanh(logits[0]),
                green + share * jnp.tanh(logits[1]),
                blue + share * jnp.tanh(logits[2]),
                later,
            )

        zero = jnp.zeros((rows, width), jnp.float32)
        red, green, blue, through = lax.fori_loop(
            0, depth_cells, cells, (zero, zero, zero, zero + 1.0), unroll=4
        )
        opacity = 1.0 - through
        out_ref[0] = 0.5 * (red + opacity)
        out_ref[1] = 0.5 * (green + opacity)
        out_ref[2] = 0.5 * (blue + opacity)
        out_ref[3] = opacity

    slots = 4 * capacity

    def render_group(number):
        copies = []
        for step in list(range(1, depth_devices)) + [0]:
            view = slab_of(step) * view_count + number
            if step == 0:
                render(view, stacks[number].at[me_d])
            else:
                render(view, images[number].at[step])
                copy = pltpu.make_async_remote_copy(
                    src_ref=images[number].at[step], dst_ref=stacks[number].at[me_d],
                    send_sem=slab_send.at[number, step], recv_sem=slab_recv.at[number, step],
                    device_id=(slab_of(step), me_r, me_c), device_id_type=MESH,
                )
                copy.start()
                copies.append(copy)
        return copies

    def composite(number):
        view = me_d * view_count + number
        stack = stacks[number]
        result = stack[order_ref[view, 0]]
        for position in range(1, depth_devices):
            result = result + (1.0 - result[3:4]) * stack[order_ref[view, position]]
        keep = lax.broadcasted_iota(jnp.int32, (rows, width), 1) < length_ref[number]
        picture = jnp.where(keep[None], result, 0.0).reshape(4 * rows, width).astype(jnp.bfloat16)
        line = lax.broadcasted_iota(jnp.int32, (tiles * slots, 4 * rows), 0)
        pixel = lax.broadcasted_iota(jnp.int32, (tiles * slots, 4 * rows), 1)
        wanted = (line // slots) * capacity + line % capacity
        key = key_by_channel_ref[number : number + 1, :]
        chosen = (wanted == key) & ((line // capacity) % 4 == pixel // rows)
        packed = jnp.dot(
            jnp.where(chosen, 1.0, 0.0).astype(jnp.bfloat16), picture, preferred_element_type=jnp.float32
        ).astype(jnp.bfloat16)
        packs[number][...] = packed.reshape(tiles, slots, width)
        arrivals[number][me_c] = packs[number][me_c]
        copies = []
        for step in range(1, tiles):
            copy = pltpu.make_async_remote_copy(
                src_ref=packs[number].at[tile_of(step)], dst_ref=arrivals[number].at[me_c],
                send_sem=tile_send.at[number, step], recv_sem=tile_recv.at[number, step],
                device_id=(me_d, me_r, tile_of(step)), device_id_type=MESH,
            )
            copy.start()
            copies.append(copy)
        return copies

    def warp(number):
        line = lax.broadcasted_iota(jnp.int32, (slots, 4 * rows), 0)
        pixel = lax.broadcasted_iota(jnp.int32, (slots, 4 * rows), 1)
        wanted = me_c * capacity + line % capacity
        same = line // capacity == pixel % 4
        places = [
            jnp.where((wanted == keys[tile, number : number + 1, :]) & same, 1.0, 0.0).astype(jnp.bfloat16)
            for tile in range(tiles)
        ]
        gathered = lax.dot_general(
            jnp.concatenate(places, axis=0),
            arrivals[number][...].reshape(tiles * slots, width),
            (((0,), (0,)), ((), ())),
            preferred_element_type=jnp.float32,
        )
        high = gathered.astype(jnp.bfloat16)
        low = (gathered - high.astype(jnp.float32)).astype(jnp.bfloat16)
        matrix = warp_ref[me_d * view_count + number]
        frame_ref[number] = jnp.dot(high, matrix, preferred_element_type=jnp.float32) + jnp.dot(
            low, matrix, preferred_element_type=jnp.float32
        )

    slab_copies, tile_copies = [], []
    for number in range(view_count):
        slab_copies.append(render_group(number))
        if number > 0:
            for copy in slab_copies[number - 1]:
                copy.wait()
            tile_copies.append(composite(number - 1))
    for copy in slab_copies[-1]:
        copy.wait()
    tile_copies.append(composite(view_count - 1))
    for copy in key_copies:
        copy.wait()
    for number in range(view_count):
        for copy in tile_copies[number]:
            copy.wait()
        warp(number)


def slot_keys(owner_rows, capacity):
    rows = owner_rows.shape[-1]
    same = owner_rows[..., :, None] == owner_rows[..., None, :]
    places = jnp.arange(rows, dtype=jnp.int32)
    rank = jnp.sum((same & (places[:, None] < places[None, :])).astype(jnp.int32), axis=-2)
    return owner_rows * capacity + rank


def body(
    species, diffusivity, reaction_rate, shear_rate, colour_weight, colour_bias,
    slab_order, lengths, owners, warp_matrix,
):
    depth_cells, rows, width = species.shape[1:]
    depth_devices = lax.axis_size("depth")
    tiles = lax.axis_size("col")
    depth_total = depth_cells * depth_devices
    rim_width = (4 * depth_total + 99) // 100
    rimmed = advance_deep(species, diffusivity, reaction_rate, rim_width)
    species_out = rimmed[:, :, :, rim_width : rim_width + width]
    views = shear_rate.shape[0]
    view_count = views // depth_devices
    capacity = 2 * rows // tiles
    cell_at = lax.axis_index("depth") * depth_cells + jnp.arange(depth_cells, dtype=jnp.int32)
    offset = shear_rate[:, None] * (cell_at.astype(jnp.float32) + 0.5 - 0.5 * depth_total)
    floor_part = jnp.floor(offset)
    fraction = offset - floor_part
    start = jnp.clip(floor_part.astype(jnp.int32) + rim_width, 0, 2 * rim_width - 1)
    halves = jnp.array([0.5, 0.5, 0.5, 1.0], jnp.float32)
    key = slot_keys(owners[:, 0, :, 0], capacity)
    key_by_channel = jnp.tile(key, (1, 4))
    key_by_row = jnp.repeat(key, 4, axis=1)
    slots = 4 * capacity
    vmem = pl.BlockSpec(memory_space=pltpu.VMEM)
    smem = pl.BlockSpec(memory_space=pltpu.SMEM)
    frame = pl.pallas_call(
        functools.partial(march_kernel, depth_devices, tiles, capacity),
        out_shape=jax.ShapeDtypeStruct((view_count, 4 * rows, width), jnp.float32),
        in_specs=[smem] * 5 + [vmem] * 5,
        out_specs=vmem,
        scratch_shapes=[pltpu.VMEM((depth_cells, 2 * rim_width, 4, rows, width), jnp.float32)]
        + [pltpu.VMEM((depth_devices, 4, rows, width), jnp.float32)] * view_count
        + [pltpu.VMEM((depth_devices, 4, rows, width), jnp.float32)] * view_count
        + [pltpu.VMEM((tiles, slots, width), jnp.bfloat16)] * view_count
        + [pltpu.VMEM((tiles, slots, width), jnp.bfloat16)] * view_count
        + [
            pltpu.VMEM((tiles, view_count, 4 * rows), jnp.int32),
            pltpu.SemaphoreType.DMA((view_count, depth_devices)),
            pltpu.SemaphoreType.DMA((view_count, depth_devices)),
            pltpu.SemaphoreType.DMA((view_count, tiles)),
            pltpu.SemaphoreType.DMA((view_count, tiles)),
            pltpu.SemaphoreType.DMA((tiles,)),
            pltpu.SemaphoreType.DMA((tiles,)),
        ],
        compiler_params=pltpu.CompilerParams(
            collective_id=1, has_side_effects=True, vmem_limit_bytes=40 * 1024 * 1024
        ),
    )(
        start, fraction, colour_weight * halves[None, :, None], colour_bias * halves, slab_order,
        rimmed, lengths[:, 0, :, None], key_by_channel, key_by_row, warp_matrix,
    )
    return (species_out, frame.reshape(view_count, rows, 4, width))


def solution(mesh):
    in_specs = (
        P(None, "depth", "row", "col"),
        P("depth", "row", "col"),
        P("depth", "row", "col"),
        P(),
        P(),
        P(),
        P(),
        P("depth", "col", "row"),
        P("depth", "col", "row", None),
        P(),
    )
    out_specs = (P(None, "depth", "row", "col"), P("depth", "row", None, "col"))
    return jax.shard_map(body, mesh=mesh, in_specs=in_specs, out_specs=out_specs, check_vma=False)
```

time: 258 us -> 91.9 us (0.36)
  waiting for transfers between devices: 69.4 us -> 18.4 us
  loops' own time: 43 us -> 0 us
  local copies, waits for them, and re-layouts: 43.7 us -> 9.95 us
  Pallas kernels: 0 us -> 30.6 us
  other arithmetic: 37.8 us -> 17.1 us
  matrix products: 19.3 us -> 0 us
  between operations: 14.6 us -> 0.98 us
  blocking collectives: 8.53 us -> 0 us
  starting transfers between devices: 19.9 us -> 14.5 us
    another operation x1 -> x0, loops' own time: 43 us -> none  [body(): lax.scan(march, start_state, jnp.arange(depth_cells, dtype=jnp.int32))]
    all_gather x1 -> x0, waiting for transfers between devices: 42.2 us -> none  [body(): everything = lax.all_gather(slab[None], 'depth', axis=0, tiled=True)]
    pallas_call x0 -> x1, Pallas kernels: none -> 30.6 us  [body(): pl.pallas_call(functools.partial(march_kernel, depth_devices, tiles, capa...]
    while x97 -> x0, local copies, waits for them, and re-layouts: 20.7 us -> none
    dot_general x19 -> x0, matrix products: 19.3 us -> none  [the longest x16 18.5 us: march(): jnp.einsum('fyp,vpx->vfyx', depth_plane, resample, precision=lax.Precisio...]
    dynamic_slice x17 -> x0, local copies, waits for them, and re-layouts: 10.8 us -> none  [the longest x16 10.7 us: body(): lax.scan(march, start_state, jnp.arange(depth_cells, dtype=jnp.int32))]
    add x66 -> x1, other arithmetic: 9.24 us -> 0.01 us  [slot_keys(): return owner_rows * capacity + rank]
    all_gather x1 -> x0, blocking collectives: 8.53 us -> none  [body(): owner_map = lax.all_gather(owners, 'col', axis=1, tiled=True)[:, :, :, 0]]
  transfers between devices with their start and end apart: 8 -> 6, of which waited for: 7 -> 4; matrix products, arithmetic and copies ran while one was open for 3% -> 6% of each run, Pallas kernels for 0% -> 0%
where the time goes in v1:
time: 91.9 us; the launch traced here: 91.5 us
  Pallas kernels  30.6 us (33%)
  waiting for transfers between devices  18.4 us (20%)
  other arithmetic  17.1 us (19%)
  starting transfers between devices  14.5 us (16%)
  local copies, waits for them, and re-layouts  9.95 us (11%)
  between operations  0.98 us (1%)
    pallas_call x1, Pallas kernels, body(): pl.pallas_call(functools.partial(march_kernel, depth_devices, tiles, capa...  30.6 us
    ppermute x3, waiting for transfers between devices, with_halo(): lax.ppermute(head, axis, [((i + 1) % count, i) for i in range(ends)])  11.8 us
    ppermute x3, starting transfers between devices, with_halo(): lax.ppermute(tail, axis, [(i, (i + 1) % count) for i in range(ends)])  10.5 us
    ppermute x3, waiting for transfers between devices, with_halo(): lax.ppermute(tail, axis, [(i, (i + 1) % count) for i in range(ends)])  6.68 us
    concatenate x2, other arithmetic, with_halo(): jnp.concatenate([lax.ppermute(tail, axis, [(i, (i + 1) % count) for i in...  4.34 us
    ppermute x3, starting transfers between devices, with_halo(): lax.ppermute(head, axis, [((i + 1) % count, i) for i in range(ends)])  4 us
    select_n x1, other arithmetic, advance_deep(): second = jnp.where(trimmed(inside, 2)[None], second, zero)  3.05 us
    slice x6, local copies, waits for them, and re-layouts, trimmed(): array[..., layers:depth_len - layers, layers:row_len - layers, layers:col...  2.97 us
  transfers between devices with their start and end apart: 6, of which 4 were waited for; matrix products, arithmetic and copies ran while one was open for 6% of the time, Pallas kernels for 0%

profile of v1, /device:TPU:0, one launch (start us, length us, event | category | flops | bytes accessed | tf_op | source)
XLA Modules:
  0.0 91.5 jit_solution(8946210726277257626)
XLA Ops:
  0.6 1.3 %pad_maximum_fusion.2 = f32[4,16,32,128]{3,2,1,0:T(8,128)S(1)} fusion(f32[1,16,32,128]{3,2,1,0:T(8,128)} %bitcast.55, f32[1,16,32,128]{3,2,1,0:T(8,128)} %bitcast.60, f32[2,16,32,128]{3,2,1,0:T(8,128)} %param.11), kind=kLoop, calls=%fused_computation.46 | loop fusion | flops 524288 | bytes 2097152 | tf_op jit(solution)/shard_map/concatenate | solution.py:74
  1.9 0.4 fusion.42
  2.3 0.0 copy-start.9
  2.3 0.0 copy-start.7
  2.3 0.0 copy-start.8
  2.3 0.0 copy-start.6
  2.4 0.0 copy-start.12
  2.4 1.1 %copy.38 = f32[4,16,32,6]{2,1,3,0:T(8,128)} copy(f32[4,16,32,6]{3,2,1,0:T(8,128)S(1)} %get-tuple-element.15) | data formatting | bytes 98304 | tf_op jit(solution)/shard_map/slice | solution.py:21
  3.5 1.4 %collective-permute-start.1 = (f32[4,16,32,6]{2,1,3,0:T(8,128)}, f32[4,16,32,6]{2,1,3,0:T(8,128)}, u32[]{:S(2)}, u32[]{:S(2)}) collective-permute-start(f32[4,16,32,6]{2,1,3,0:T(8,128)} %copy.38), channel_id=1, source_target_pairs={{1,0},{2,1},{3,2},{5,4},{6,5},{7,6},{9,8},{10,9},{11,10},{13,12},{... | collective-permute-start | bytes 147464 | tf_op jit(solution)/shard_map/ppermute | solution.py:27
  4.9 0.5 copy.37
  5.4 5.6 %collective-permute-start = (f32[4,16,32,6]{2,1,3,0:T(8,128)S(1)}, f32[4,16,32,6]{2,1,3,0:T(8,128)S(1)}, u32[]{:S(2)}, u32[]{:S(2)}) collective-permute-start(f32[4,16,32,6]{2,1,3,0:T(8,128)S(1)} %copy.37), channel_id=1, source_target_pairs={{0,1},{1,2},{2,3},{4,5},{5,6},{6,7},{8,9},{9,10},{10,11},{12,13},{... | collective-permute-start | bytes 147464 | tf_op jit(solution)/shard_map/ppermute | solution.py:25
  11.1 0.1 copy.43
  11.2 0.0 copy-done.7
  11.2 0.1 copy.41
  11.3 0.1 broadcast_multiply_fusion.weight_ref
  11.4 0.1 broadcast_and_fusion.1
  11.5 0.1 convert_reduce_fusion
  11.6 0.1 floor_subtract_fusion.fraction_ref
  11.7 0.2 broadcast_and_fusion
  11.9 0.9 slice.209
  12.7 1.0 %slice.213 = pred[18,34,136]{2,1,0:T(8,128)(4,1)} slice(pred[22,38,140]{2,1,0:T(8,128)(4,1)S(1)} %broadcast_and_fusion), slice={[2:20], [2:36], [2:138]} | slice | bytes 166464 | tf_op jit(solution)/shard_map/slice | solution.py:60
  13.7 0.3 slice.215
  14.1 0.1 tile.10.key_by_channel_ref
  14.2 0.0 copy-done.10
  14.2 0.1 copy.45.order_ref
  14.3 0.1 broadcast_in_dim.69
  14.3 0.1 reshape.103.key_by_row_ref
  14.5 0.1 copy.46.length_ref
  14.6 0.6 collective-permute-done
  15.1 0.5 copy.39
  15.6 0.0 collective-permute-done.1
  15.6 1.4 %copy.40 = f32[4,16,32,6]{3,2,1,0:T(8,128)S(1)} copy(f32[4,16,32,6]{2,1,3,0:T(8,128)} %collective-permute-done.1) | data formatting | bytes 98304 | tf_op jit(solution)/shard_map/ppermute | solution.py:27
  17.0 0.0 copy-done.2
  17.0 0.0 copy-done.3
  17.0 0.4 pad_maximum_fusion.4
  17.4 3.6 %collective-permute-start.2 = (f32[4,3,32,140]{3,2,1,0:T(8,128)S(1)}, f32[4,3,32,140]{3,2,1,0:T(8,128)S(1)}, u32[]{:S(2)}, u32[]{:S(2)}) collective-permute-start(f32[4,3,32,140]{3,2,1,0:T(8,128)S(1)} %get-tuple-element.12), channel_id=1, source_target_pairs={{0,8},{8,16},{16,24},{1,9},{9,17},{17,25},{2,10},{10,18},{18,26},{... | collective-permute-start | bytes 645128 | tf_op jit(solution)/shard_map/ppermute | solution.py:25
  21.0 1.3 %collective-permute-start.3 = (f32[4,3,32,140]{3,2,1,0:T(8,128)S(1)}, f32[4,3,32,140]{3,2,1,0:T(8,128)S(1)}, u32[]{:S(2)}, u32[]{:S(2)}) collective-permute-start(f32[4,3,32,140]{3,2,1,0:T(8,128)S(1)} %get-tuple-element.13), channel_id=1, source_target_pairs={{8,0},{16,8},{24,16},{9,1},{17,9},{25,17},{10,2},{18,10},{26,18},{... | collective-permute-start | bytes 645128 | tf_op jit(solution)/shard_map/ppermute | solution.py:27
  22.3 0.1 fusion.38.start_ref
  22.3 6.1 %collective-permute-done.2 = f32[4,3,32,140]{3,2,1,0:T(8,128)S(1)} collective-permute-done((f32[4,3,32,140]{3,2,1,0:T(8,128)S(1)}, f32[4,3,32,140]{3,2,1,0:T(8,128)S(1)}, u32[]{:S(2)}, u32[]{:S(2)}) %collective-permute-start.2) | collective-permute-done | bytes 215072 | tf_op jit(solution)/shard_map/ppermute | solution.py:25
  28.5 10.4 %collective-permute-done.3 = f32[4,3,32,140]{3,2,1,0:T(8,128)S(1)} collective-permute-done((f32[4,3,32,140]{3,2,1,0:T(8,128)S(1)}, f32[4,3,32,140]{3,2,1,0:T(8,128)S(1)}, u32[]{:S(2)}, u32[]{:S(2)}) %collective-permute-start.3) | collective-permute-done | bytes 215072 | tf_op jit(solution)/shard_map/ppermute | solution.py:27
  38.8 0.5 pad_maximum_fusion.11
  39.3 1.3 %collective-permute-start.4 = (f32[4,22,3,140]{3,2,1,0:T(4,128)S(1)}, f32[4,22,3,140]{3,2,1,0:T(4,128)S(1)}, u32[]{:S(2)}, u32[]{:S(2)}) collective-permute-start(f32[4,22,3,140]{3,2,1,0:T(4,128)S(1)} %get-tuple-element.8), channel_id=1, source_target_pairs={{0,4},{1,5},{2,6},{3,7},{8,12},{9,13},{10,14},{11,15},{16,20},{17,... | collective-permute-start | bytes 443528 | tf_op jit(solution)/shard_map/ppermute | solution.py:25
  40.6 1.3 %collective-permute-start.5 = (f32[4,22,3,140]{3,2,1,0:T(4,128)S(1)}, f32[4,22,3,140]{3,2,1,0:T(4,128)S(1)}, u32[]{:S(2)}, u32[]{:S(2)}) collective-permute-start(f32[4,22,3,140]{3,2,1,0:T(4,128)S(1)} %get-tuple-element.9), channel_id=1, source_target_pairs={{4,0},{5,1},{6,2},{7,3},{12,8},{13,9},{14,10},{15,11},{20,16},{21,... | collective-permute-start | bytes 443528 | tf_op jit(solution)/shard_map/ppermute | solution.py:27
  41.9 0.9 pad_maximum_fusion.1
  42.8 0.0 collective-permute-done.4
  42.8 1.4 %collective-permute-done.5 = f32[4,22,3,140]{3,2,1,0:T(4,128)S(1)} collective-permute-done((f32[4,22,3,140]{3,2,1,0:T(4,128)S(1)}, f32[4,22,3,140]{3,2,1,0:T(4,128)S(1)}, u32[]{:S(2)}, u32[]{:S(2)}) %collective-permute-start.5) | collective-permute-done | bytes 147872 | tf_op jit(solution)/shard_map/ppermute | solution.py:27
  44.2 3.5 %pad_maximum_fusion = f32[4,22,38,140]{3,2,1,0:T(8,128)S(1)} fusion(f32[4,22,3,140]{3,2,1,0:T(4,128)S(1)} %collective-permute-done.5, f32[4,3,32,140]{3,2,1,0:T(8,128)S(1)} %collective-permute-done.3, f32[4,16,32,6]{3,2,1,0:T(8,128)S(1)} %copy.40, f32[1,16,32,128]{3,2,1,0:T(8,128)S(1)} %bitcast.59, f32[1,16,32,128]{3,2,1,0:T(8,128)S(1)} %bitcast.64, ...), kind=kLoop, calls=%fused_computation | loop fusion | flops 3745280 | bytes 3745280 | tf_op jit(solution)/shard_map/concatenate | solution.py:23
  47.7 0.1 slice_bitcast_fusion.1
  47.8 0.2 slice.241
  48.0 0.3 slice.230
  48.3 0.3 slice.218
  48.6 0.8 negate_bitcast_fusion
  49.3 2.9 %fusion.6 = f32[2,20,36,138]{3,2,1,0:T(8,128)S(1)} fusion(f32[4,22,38,140]{3,2,1,0:T(8,128)S(1)} %pad_maximum_fusion, f32[1,20,36,138]{3,2,1,0:T(8,128)S(1)} %bitcast.65, f32[1,20,36,138]{3,2,1,0:T(8,128)S(1)} %get-tuple-element.6, f32[20,36,138]{2,1,0:T(8,128)S(1)} %slice.218, pred[20,36,138]{2,1,0:T(8,128)(4,1)S(1)} %slice.215), kind=kLoop, calls=%fused_computation.9 | loop fusion | flops 4371840 | bytes 7650720 | tf_op jit(solution)/shard_map/jit(_where)/select_n | solution.py:92
  52.3 0.0 copy-start.4
  52.3 0.7 negate_bitcast_fusion.1
  53.0 0.2 copy-done.4
  53.2 3.0 %fusion.17 = f32[2,18,34,136]{3,2,1,0:T(8,128)S(1)} fusion(f32[2,20,36,138]{3,2,1,0:T(8,128)S(1)} %fusion.6, f32[4,22,38,140]{3,2,1,0:T(8,128)S(1)} %pad_maximum_fusion, f32[1,18,34,136]{3,2,1,0:T(8,128)S(1)} %bitcast.66, f32[1,18,34,136]{3,2,1,0:T(8,128)S(1)} %get-tuple-element.4, f32[18,34,136]{2,1,0:T(8,128)S(1)} %slice.230, ...), kind=kLoop, calls=%fused_computation.23 | loop fusion | flops 4161600 | bytes 7074720 | tf_op jit(solution)/shard_map/jit(_where)/select_n | solution.py:96
  56.3 0.5 negate_bitcast_fusion.2
  56.8 0.4 copy-done.5
  57.2 2.0 %fusion.28.rimmed_ref = f32[2,16,32,134]{3,2,1,0:T(8,128)S(1)} fusion(f32[2,18,34,136]{3,2,1,0:T(8,128)S(1)} %fusion.17, f32[4,16,32,140]{3,2,1,0:T(8,128)S(1)} %pad_maximum_fusion.1, f32[1,16,32,134]{3,2,1,0:T(8,128)S(1)} %bitcast.67, f32[1,16,32,134]{3,2,1,0:T(8,128)S(1)} %get-tuple-element.2, f32[16,32,134]{2,1,0:T(8,128)S(1)} %slice.241, ...), kind=kLoop, calls=%fused_computation.40 | loop fusion | flops 3430400 | bytes 5831680 | tf_op jit(solution)/shard_map/jit(_where)/select_n | solution.py:100
  59.2 1.0 %slice.251 = f32[2,16,32,128]{3,2,1,0:T(8,128)} slice(f32[2,16,32,134]{3,2,1,0:T(8,128)S(1)} %fusion.28.rimmed_ref), slice={[0:2], [0:16], [0:32], [3:131]} | slice | bytes 1048576 | tf_op jit(solution)/shard_map/slice | solution.py:296
  60.2 0.0 copy-done
  60.2 30.6 %shard_map.122 = f32[4,128,128]{2,1,0:T(8,128)S(1)} custom-call(s32[16,16]{1,0:T(8,128)S(1)} %fusion.38.start_ref, f32[16,16]{1,0:T(8,128)S(1)} %floor_subtract_fusion.fraction_ref, f32[16,4,2]{2,1,0:T(4,128)S(1)} %broadcast_multiply_fusion.weight_ref, f32[16,4]{1,0:T(8,128)S(1)} %broadcast_multiply_fusion.1.bias_ref, s32[16,4]{1,0:T(8,128)S(1)} %copy.45.order_ref, ...), custom_call_target="tpu_custom_call" | custom-call | tf_op jit(solution)/shard_map/pallas_call | solution.py:312
  90.8 0.7 copy.48
  (21 shorter events, 0.1 us)
Async XLA Ops:
  2.3 8.8 %copy-start.9 = (f32[16,4]{0,1:T(4,128)S(1)}, f32[16,4]{0,1:T(4,128)}, u32[]{:S(2)}) copy-start(f32[16,4]{0,1:T(4,128)} %param.16) | copy-start | bytes 772
  2.3 8.9 %copy-start.7 = (f32[16,4,2]{0,2,1:T(2,128)S(1)}, f32[16,4,2]{0,2,1:T(2,128)}, u32[]{:S(2)}) copy-start(f32[16,4,2]{0,2,1:T(2,128)} %param.15) | copy-start | bytes 1540
  2.3 9.0 %copy-start.8 = (f32[4]{0:T(128)S(1)}, f32[4]{0:T(128)}, u32[]{:S(2)}) copy-start(f32[4]{0:T(128)} %constant.18.clone) | copy-start | bytes 52
  2.3 9.1 %copy-start.6 = (s32[4,1,32,1]{2,3,1,0:T(1,128)S(1)}, s32[4,1,32,1]{2,3,1,0:T(1,128)}, u32[]{:S(2)}) copy-start(s32[4,1,32,1]{2,3,1,0:T(1,128)} %param.19) | copy-start | bytes 1540
  2.4 9.2 %copy-start.12 = (f32[16]{0:T(128)S(1)}, f32[16]{0:T(128)}, u32[]{:S(2)}) copy-start(f32[16]{0:T(128)} %param.14) | copy-start | bytes 196
  3.5 10.7 %copy-start.10 = (s32[16,4]{0,1:T(4,128)S(1)}, s32[16,4]{0,1:T(4,128)}, u32[]{:S(2)}) copy-start(s32[16,4]{0,1:T(4,128)} %param.17) | copy-start | bytes 772
  3.5 10.9 %copy-start.11 = (s32[4,1,32]{2,1,0:T(1,128)S(1)}, s32[4,1,32]{2,1,0:T(1,128)}, u32[]{:S(2)}) copy-start(s32[4,1,32]{2,1,0:T(1,128)} %param.18) | copy-start | bytes 1540
  3.5 12.1 %collective-permute-start.1 = (f32[4,16,32,6]{2,1,3,0:T(8,128)}, f32[4,16,32,6]{2,1,3,0:T(8,128)}, u32[]{:S(2)}, u32[]{:S(2)}) collective-permute-start(f32[4,16,32,6]{2,1,3,0:T(8,128)} %copy.38), channel_id=1, source_target_pairs={{1,0},{2,1},{3,2},{5,4},{6,5},{7,6},{9,8},{10,9},{11,10},{13,12},{... | collective-permute-start | bytes 147464 | tf_op jit(solution)/shard_map/ppermute | solution.py:27
  5.4 9.7 %collective-permute-start = (f32[4,16,32,6]{2,1,3,0:T(8,128)S(1)}, f32[4,16,32,6]{2,1,3,0:T(8,128)S(1)}, u32[]{:S(2)}, u32[]{:S(2)}) collective-permute-start(f32[4,16,32,6]{2,1,3,0:T(8,128)S(1)} %copy.37), channel_id=1, source_target_pairs={{0,1},{1,2},{2,3},{4,5},{5,6},{6,7},{8,9},{9,10},{10,11},{12,13},{... | collective-permute-start | bytes 147464 | tf_op jit(solution)/shard_map/ppermute | solution.py:25
  13.7 3.3 %copy-start.1 = (f32[2,16,32,128]{3,2,1,0:T(8,128)S(1)}, f32[2,16,32,128]{3,2,1,0:T(8,128)}, u32[]{:S(2)}) copy-start(f32[2,16,32,128]{3,2,1,0:T(8,128)} %param.11) | copy-start | bytes 1572868
  13.7 3.3 %copy-start.2 = (f32[16,32,128]{2,1,0:T(8,128)S(1)}, f32[16,32,128]{2,1,0:T(8,128)}, u32[]{:S(2)}) copy-start(f32[16,32,128]{2,1,0:T(8,128)} %param.13) | copy-start | bytes 786436
  13.7 3.3 %copy-start.3 = (f32[16,32,128]{2,1,0:T(8,128)S(1)}, f32[16,32,128]{2,1,0:T(8,128)}, u32[]{:S(2)}) copy-start(f32[16,32,128]{2,1,0:T(8,128)} %param.12) | copy-start | bytes 786436
  17.4 11.1 %collective-permute-start.2 = (f32[4,3,32,140]{3,2,1,0:T(8,128)S(1)}, f32[4,3,32,140]{3,2,1,0:T(8,128)S(1)}, u32[]{:S(2)}, u32[]{:S(2)}) collective-permute-start(f32[4,3,32,140]{3,2,1,0:T(8,128)S(1)} %get-tuple-element.12), channel_id=1, source_target_pairs={{0,8},{8,16},{16,24},{1,9},{9,17},{17,25},{2,10},{10,18},{18,26},{... | collective-permute-start | bytes 645128 | tf_op jit(solution)/shard_map/ppermute | solution.py:25
  21.0 17.9 %collective-permute-start.3 = (f32[4,3,32,140]{3,2,1,0:T(8,128)S(1)}, f32[4,3,32,140]{3,2,1,0:T(8,128)S(1)}, u32[]{:S(2)}, u32[]{:S(2)}) collective-permute-start(f32[4,3,32,140]{3,2,1,0:T(8,128)S(1)} %get-tuple-element.13), channel_id=1, source_target_pairs={{8,0},{16,8},{24,16},{9,1},{17,9},{25,17},{10,2},{18,10},{26,18},{... | collective-permute-start | bytes 645128 | tf_op jit(solution)/shard_map/ppermute | solution.py:27
  39.3 3.5 %collective-permute-start.4 = (f32[4,22,3,140]{3,2,1,0:T(4,128)S(1)}, f32[4,22,3,140]{3,2,1,0:T(4,128)S(1)}, u32[]{:S(2)}, u32[]{:S(2)}) collective-permute-start(f32[4,22,3,140]{3,2,1,0:T(4,128)S(1)} %get-tuple-element.8), channel_id=1, source_target_pairs={{0,4},{1,5},{2,6},{3,7},{8,12},{9,13},{10,14},{11,15},{16,20},{17,... | collective-permute-start | bytes 443528 | tf_op jit(solution)/shard_map/ppermute | solution.py:25
  40.6 3.6 %collective-permute-start.5 = (f32[4,22,3,140]{3,2,1,0:T(4,128)S(1)}, f32[4,22,3,140]{3,2,1,0:T(4,128)S(1)}, u32[]{:S(2)}, u32[]{:S(2)}) collective-permute-start(f32[4,22,3,140]{3,2,1,0:T(4,128)S(1)} %get-tuple-element.9), channel_id=1, source_target_pairs={{4,0},{5,1},{6,2},{7,3},{12,8},{13,9},{14,10},{15,11},{20,16},{21,... | collective-permute-start | bytes 443528 | tf_op jit(solution)/shard_map/ppermute | solution.py:27
  52.3 0.9 %copy-start.4 = (pred[18,34,136]{2,1,0:T(8,128)(4,1)S(1)}, pred[18,34,136]{2,1,0:T(8,128)(4,1)}, u32[]{:S(2)}) copy-start(pred[18,34,136]{2,1,0:T(8,128)(4,1)} %slice.213) | copy-start | bytes 249700
  56.3 0.9 copy-start.5
  57.2 3.0 %copy-start = (bf16[16,128,128]{2,1,0:T(8,128)(2,1)S(1)}, bf16[16,128,128]{2,1,0:T(8,128)(2,1)}, u32[]{:S(2)}) copy-start(bf16[16,128,128]{2,1,0:T(8,128)(2,1)} %warp_ref.1) | copy-start | bytes 1572868

commit v2 on v1

--- a/solution.py
+++ b/solution.py
@@ -14,101 +14,264 @@
 VEL_COL = 0.4
 
 
-def with_halo(cells, sides, width):
-    for axis, dim in sides:
-        count = lax.axis_size(axis)
-        ends = count - 1
-        head = lax.slice_in_dim(cells, 0, width, axis=dim)
-        tail = lax.slice_in_dim(cells, cells.shape[dim] - width, cells.shape[dim], axis=dim)
-        cells = jnp.concatenate(
-            [
-                lax.ppermute(tail, axis, [(i, (i + 1) % count) for i in range(ends)]),
-                cells,
-                lax.ppermute(head, axis, [((i + 1) % count, i) for i in range(ends)]),
-            ],
-            axis=dim,
+MESH = pl.DeviceIdType.MESH
+
+LAYERS = 3
+
+
+def advance(
+    depth_devices, row_devices, tiles, rim_width,
+    species_ref, diffusivity_ref, rate_ref, species_out_ref, shifted,
+    deep, first_ref, second_ref, step_ref, row_got, packs, got, stage_out, stage_in, send_sem, recv_sem,
+):
+    me_d, me_r, me_c = lax.axis_index("depth"), lax.axis_index("row"), lax.axis_index("col")
+    depth_cells, rows, width = species_ref.shape[1:]
+    tall, wide = rows + 8, 2 * width
+    edge = LAYERS + rim_width
+    last = LAYERS + depth_cells
+
+    def link(number, src, dst, device):
+        return pltpu.make_async_remote_copy(
+            src_ref=src, dst_ref=dst, send_sem=send_sem.at[number], recv_sem=recv_sem.at[number],
+            device_id=device, device_id_type=MESH,
         )
-    return cells
-
-
-def tendency_of(padded, diffusivity, reaction_rate):
-    centre = padded[:, 1:-1, 1:-1, 1:-1]
-    below_depth = padded[:, :-2, 1:-1, 1:-1]
-    above_depth = padded[:, 2:, 1:-1, 1:-1]
-    below_row = padded[:, 1:-1, :-2, 1:-1]
-    above_row = padded[:, 1:-1, 2:, 1:-1]
-    below_col = padded[:, 1:-1, 1:-1, :-2]
-    above_col = padded[:, 1:-1, 1:-1, 2:]
-    laplace = (
-        below_depth + above_depth + below_row + above_row + below_col + above_col - 6.0 * centre
-    )
-    advect = (
-        VEL_DEPTH * (centre - below_depth)
-        + VEL_ROW * (centre - below_row)
-        + VEL_COL * (centre - below_col)
-    )
-    heat_part = centre[1]
-    burned = reaction_rate * centre[0] * heat_part * heat_part / (1.0 + heat_part * heat_part)
-    source = jnp.stack([-burned, burned])
-    return diffusivity * laplace - advect + source
-
-
-def trimmed(array, layers):
-    depth_len = array.shape[-3]
-    row_len = array.shape[-2]
-    col_len = array.shape[-1]
-    return array[
-        ..., layers : depth_len - layers, layers : row_len - layers, layers : col_len - layers
+
+    def begin(place, count, down, up):
+        @pl.when(place > 0)
+        def _():
+            for copy in down:
+                copy.start()
+
+        @pl.when(place < count - 1)
+        def _():
+            for copy in up:
+                copy.start()
+
+    def finish(place, count, down, up, below, above):
+        @pl.when(place > 0)
+        def _():
+            for copy in down:
+                copy.wait_send()
+            for copy in up:
+                copy.wait_recv()
+
+        @pl.when(place < count - 1)
+        def _():
+            for copy in up:
+                copy.wait_send()
+            for copy in down:
+                copy.wait_recv()
+
+        @pl.when(place == 0)
+        def _():
+            below[...] = jnp.zeros(below.shape, below.dtype)
+
+        @pl.when(place == count - 1)
+        def _():
+            above[...] = jnp.zeros(above.shape, above.dtype)
+
+    row_down = (me_d, lax.rem(me_r + row_devices - 1, row_devices), me_c)
+    row_up = (me_d, lax.rem(me_r + 1, row_devices), me_c)
+    col_down = (me_d, me_r, lax.rem(me_c + tiles - 1, tiles))
+    col_up = (me_d, me_r, lax.rem(me_c + 1, tiles))
+    depth_down = (lax.rem(me_d + depth_devices - 1, depth_devices), me_r, me_c)
+    depth_up = (lax.rem(me_d + 1, depth_devices), me_r, me_c)
+
+    low, high = pl.ds(0, 8), pl.ds(rows - 8, 8)
+    down = [
+        link(0, species_ref.at[:, :, low], row_got.at[1, pl.ds(0, 2)], row_down),
+        link(1, diffusivity_ref.at[:, low], row_got.at[1, 2], row_down),
+        link(2, rate_ref.at[:, low], row_got.at[1, 3], row_down),
     ]
-
-
-def inside_grid(first_index, count, margin, total):
-    places = first_index - margin + jnp.arange(count + 2 * margin, dtype=jnp.int32)
-    return (places >= 0) & (places < total)
-
-
-def advance_deep(species, diffusivity, reaction_rate, rim_width):
-    depth_cells = species.shape[1]
-    rows = species.shape[2]
-    width = species.shape[3]
-    packed = jnp.concatenate([species, diffusivity[None], reaction_rate[None]], axis=0)
-    wide = with_halo(packed, (("col", 3),), 3 + rim_width)
-    deep = with_halo(wide, (("depth", 1), ("row", 2)), 3)
-    depth_ok = inside_grid(
-        lax.axis_index("depth") * depth_cells, depth_cells, 3, depth_cells * lax.axis_size("depth")
-    )
-    row_ok = inside_grid(lax.axis_index("row") * rows, rows, 3, rows * lax.axis_size("row"))
-    col_ok = inside_grid(
-        lax.axis_index("col") * width, width, 3 + rim_width, width * lax.axis_size("col")
-    )
-    inside = depth_ok[:, None, None] & row_ok[None, :, None] & col_ok[None, None, :]
-    fields = deep[:2]
-    spread = deep[2]
-    rates = deep[3]
-    zero = jnp.zeros((), jnp.float32)
-    first = trimmed(fields, 1) + TIME_STEP * tendency_of(
-        fields, trimmed(spread, 1), trimmed(rates, 1)
-    )
-    first = jnp.where(trimmed(inside, 1)[None], first, zero)
-    second = 0.75 * trimmed(fields, 2) + 0.25 * (
-        trimmed(first, 1) + TIME_STEP * tendency_of(first, trimmed(spread, 2), trimmed(rates, 2))
-    )
-    second = jnp.where(trimmed(inside, 2)[None], second, zero)
-    final = trimmed(fields, 3) / 3.0 + 2.0 / 3.0 * (
-        trimmed(second, 1) + TIME_STEP * tendency_of(second, trimmed(spread, 3), trimmed(rates, 3))
-    )
-    final = jnp.where(trimmed(inside, 3)[None], final, zero)
-    return final
-
-
-MESH = pl.DeviceIdType.MESH
+    up = [
+        link(3, species_ref.at[:, :, high], row_got.at[0, pl.ds(0, 2)], row_up),
+        link(4, diffusivity_ref.at[:, high], row_got.at[0, 2], row_up),
+        link(5, rate_ref.at[:, high], row_got.at[0, 3], row_up),
+    ]
+    begin(me_r, row_devices, down, up)
+
+    def place_cells(cell, carry):
+        for field in range(2):
+            deep[field, LAYERS + cell, pl.ds(0, rows), pl.ds(0, width)] = species_ref[field, cell]
+        deep[2, LAYERS + cell, pl.ds(0, rows), pl.ds(0, width)] = diffusivity_ref[cell]
+        deep[3, LAYERS + cell, pl.ds(0, rows), pl.ds(0, width)] = rate_ref[cell]
+        return carry
+
+    lax.fori_loop(0, depth_cells, place_cells, 0)
+    row_at = lax.broadcasted_iota(jnp.int32, (tall, wide), 0)
+    row_at = me_r * rows + jnp.where(row_at < rows + 4, row_at, row_at - tall)
+    col_at = lax.broadcasted_iota(jnp.int32, (tall, wide), 1)
+    col_at = me_c * width + jnp.where(col_at < width + width // 2, col_at, col_at - wide)
+    inside = (row_at >= 0) & (row_at < rows * row_devices) & (col_at >= 0) & (col_at < width * tiles)
+    step_ref[...] = jnp.where(inside, TIME_STEP, 0.0)
+    finish(me_r, row_devices, down, up, row_got.at[0], row_got.at[1])
+
+    near = lax.broadcasted_iota(jnp.int32, (8, width), 0) < 4
+
+    def place_rows(cell, carry):
+        for field in range(4):
+            deep[field, LAYERS + cell, pl.ds(rows, 8), pl.ds(0, width)] = jnp.where(
+                near, row_got[1, field, cell], row_got[0, field, cell]
+            )
+        return carry
+
+    lax.fori_loop(0, depth_cells, place_rows, 0)
+
+    lane = lax.broadcasted_iota(jnp.int32, (tall, width), 1)
+
+    def turned(array, shift):
+        shift = shift % width
+        return array if shift == 0 else pltpu.roll(array, shift, 1)
+
+    def pack_columns(field, carry):
+        left = jnp.zeros((tall, width), jnp.float32)
+        right = left
+        for cell in range(depth_cells):
+            plane = deep[field, LAYERS + cell, :, pl.ds(0, width)]
+            here = (lane >= edge * cell) & (lane < edge * (cell + 1))
+            left = jnp.where(here, turned(plane, edge * cell), left)
+            right = jnp.where(here, turned(plane, edge * (cell + 1)), right)
+        packs[0, field] = left
+        packs[1, field] = right
+        return carry
+
+    lax.fori_loop(0, 4, pack_columns, 0)
+    down = [link(6, packs.at[0], got.at[1], col_down)]
+    up = [link(7, packs.at[1], got.at[0], col_up)]
+    begin(me_c, tiles, down, up)
+    finish(me_c, tiles, down, up, got.at[0], got.at[1])
+
+    def side_tile(below, below_at, above, above_at):
+        return jnp.where(
+            lane < edge,
+            turned(above, -above_at),
+            jnp.where(lane >= width - edge, turned(below, width - edge - below_at), 0.0),
+        )
+
+    lower = [(f, LAYERS + k, last + k) for f in range(2) for k in range(3)]
+    lower += [(f, LAYERS + k, last + k) for f in range(2, 4) for k in range(2)]
+    upper = [(f, last - 3 + k, k) for f in range(2) for k in range(3)]
+    upper += [(f, last - 3 + k, k) for f in range(2, 4) for k in range(1, 3)]
+    span = 3 * edge
+
+    def corner_at(field, side):
+        return (field % 2) * (width // 2) + side * (width // 4)
+
+    for way, (items, start) in enumerate(((lower, 0), (upper, edge * (depth_cells - 3)))):
+        for pair in range(len(items) // 2):
+            planes = [deep[f, here, :, pl.ds(0, width)] for f, here, _ in items[2 * pair : 2 * pair + 2]]
+            stage_out[way, pair] = jnp.concatenate(planes, axis=0).astype(jnp.bfloat16)
+        corners = []
+        for half in range(2):
+            tile = jnp.zeros((tall, width), jnp.float32)
+            for field in (2 * half, 2 * half + 1):
+                for side in range(2):
+                    at = corner_at(field, side)
+                    here = (lane >= at) & (lane < at + span)
+                    tile = jnp.where(here, turned(got[side, field], at - start), tile)
+            corners.append(tile)
+        stage_out[way, len(items) // 2] = jnp.concatenate(corners, axis=0).astype(jnp.bfloat16)
+    down = [link(8, stage_out.at[0], stage_in.at[1], depth_down)]
+    up = [link(9, stage_out.at[1], stage_in.at[0], depth_up)]
+    begin(me_d, depth_devices, down, up)
+
+    def place_sides(field, carry):
+        for cell in range(depth_cells):
+            deep[field, LAYERS + cell, :, pl.ds(width, width)] = side_tile(
+                got[0, field], edge * cell, got[1, field], edge * cell
+            )
+        return carry
+
+    lax.fori_loop(0, 4, place_sides, 0)
+
+    def rates_of(source, plane):
+        time_step = step_ref[...]
+        at = me_d * depth_cells + plane - LAYERS
+        time_step = time_step * jnp.where((at >= 0) & (at < depth_cells * depth_devices), 1.0, 0.0)
+        fuel, heat = source[0, plane], source[1, plane]
+        squared = heat * heat
+        burned = deep[3, plane] * fuel * squared / (1.0 + squared)
+        spread = deep[2, plane]
+        changes = []
+        for field, centre in ((0, fuel), (1, heat)):
+            below_depth, above_depth = source[field, plane - 1], source[field, plane + 1]
+            below_row, above_row = pltpu.roll(centre, 1, 0), pltpu.roll(centre, tall - 1, 0)
+            below_col, above_col = pltpu.roll(centre, 1, 1), pltpu.roll(centre, wide - 1, 1)
+            laplace = (
+                below_depth + above_depth + below_row + above_row + below_col + above_col - 6.0 * centre
+            )
+            carried = (
+                VEL_DEPTH * below_depth + VEL_ROW * below_row + VEL_COL * below_col
+                - (VEL_DEPTH + VEL_ROW + VEL_COL) * centre
+            )
+            total = spread * laplace + carried
+            total = total - burned if field == 0 else total + burned
+            changes.append(centre + time_step * total)
+        return changes
+
+    def first_stage(plane):
+        for field, value in enumerate(rates_of(deep, plane)):
+            first_ref[field, plane] = value
+
+    def second_stage(plane):
+        for field, value in enumerate(rates_of(first_ref, plane)):
+            second_ref[field, plane] = 0.75 * deep[field, plane] + 0.25 * value
+
+    def third_stage(plane):
+        cell = plane - LAYERS
+        for field, value in enumerate(rates_of(second_ref, plane)):
+            final = deep[field, plane] * (1.0 / 3.0) + (2.0 / 3.0) * value
+            final = final[:rows]
+            species_out_ref[field, cell] = final[:, :width]
+            earlier = pltpu.roll(final, rim_width, 1)[:, :width]
+            for shift in range(2 * rim_width):
+                turn = (rim_width - shift - 1) % wide
+                later = (final if turn == 0 else pltpu.roll(final, turn, 1))[:, :width]
+                shifted[cell, shift, 2 * field] = earlier
+                shifted[cell, shift, 2 * field + 1] = later - earlier
+                earlier = later
+
+    def inner(stage, begin_at, end_at):
+        def one(plane, carry):
+            stage(plane)
+            return carry
+
+        lax.fori_loop(begin_at, end_at, one, 0)
+
+    def outer(stage, begin_at, gap):
+        def one(number, carry):
+            stage(begin_at + number + (number // 3) * gap)
+            return carry
+
+        lax.fori_loop(0, 6, one, 0)
+
+    inner(first_stage, LAYERS + 1, last - 1)
+    inner(second_stage, LAYERS + 2, last - 2)
+    inner(third_stage, LAYERS + 3, last - 3)
+    finish(me_d, depth_devices, down, up, stage_in.at[0], stage_in.at[1])
+    for way, (items, place) in enumerate(((upper, 0), (lower, last))):
+        pairs = len(items) // 2
+        corners = stage_in[way, pairs].astype(jnp.float32)
+        for pair in range(pairs):
+            both = stage_in[way, pair].astype(jnp.float32)
+            for half in range(2):
+                field, _, there = items[2 * pair + half]
+                deep[field, there, :, pl.ds(0, width)] = both[half * tall : (half + 1) * tall]
+                tile = corners[field // 2 * tall : (field // 2 + 1) * tall]
+                layer = edge * (there - place)
+                deep[field, there, :, pl.ds(width, width)] = side_tile(
+                    tile, corner_at(field, 0) + layer, tile, corner_at(field, 1) + layer
+                )
+    outer(first_stage, 1, depth_cells - 2)
+    outer(second_stage, 2, depth_cells - 4)
+    outer(third_stage, 3, depth_cells - 6)
 
 
 def march_kernel(
-    depth_devices, tiles, capacity,
+    depth_devices, row_devices, tiles, capacity, rim_width,
     start_ref, fraction_ref, weight_ref, bias_ref, order_ref,
-    rimmed_ref, length_ref, key_by_channel_ref, key_by_row_ref, warp_ref,
-    frame_ref,
+    species_ref, diffusivity_ref, rate_ref, length_ref, key_by_channel_ref, key_by_row_ref, warp_ref,
+    species_out_ref, frame_ref,
     shifted, *scratch,
 ):
     view_count = frame_ref.shape[0]
@@ -116,9 +279,11 @@
     images = scratch[view_count : 2 * view_count]
     packs = scratch[2 * view_count : 3 * view_count]
     arrivals = scratch[3 * view_count : 4 * view_count]
-    keys, slab_send, slab_recv, tile_send, tile_recv, key_send, key_recv = scratch[4 * view_count :]
+    keys, slab_send, slab_recv, tile_send, tile_recv, key_send, key_recv = scratch[
+        4 * view_count : 4 * view_count + 7
+    ]
+    advance_scratch = scratch[4 * view_count + 7 :]
     depth_cells, rows, width = shifted.shape[0], shifted.shape[3], shifted.shape[4]
-    shifts = shifted.shape[1]
     me_d, me_r, me_c = lax.axis_index("depth"), lax.axis_index("row"), lax.axis_index("col")
 
     def slab_of(step):
@@ -133,17 +298,11 @@
     for step in range(1, tiles):
         pl.semaphore_signal(barrier, inc=1, device_id=(me_d, me_r, tile_of(step)), device_id_type=MESH)
 
-    def shift_planes(cell, carry):
-        for field in range(2):
-            plane = rimmed_ref[field, cell]
-            for shift in range(shifts):
-                here = plane[:, shift : shift + width]
-                shifted[cell, shift, 2 * field] = here
-                shifted[cell, shift, 2 * field + 1] = plane[:, shift + 1 : shift + 1 + width] - here
-        return carry
-
-    lax.fori_loop(0, depth_cells, shift_planes, 0)
-    pl.semaphore_wait(barrier, depth_devices - 1 + tiles - 1)
+    row_steps = sorted({1, row_devices - 1})
+    for step in row_steps:
+        row_peer = lax.rem(me_r + step, row_devices)
+        pl.semaphore_signal(barrier, inc=1, device_id=(me_d, row_peer, me_c), device_id_type=MESH)
+    pl.semaphore_wait(barrier, depth_devices - 1 + tiles - 1 + len(row_steps))
 
     key_copies = []
     for step in range(1, tiles):
@@ -155,6 +314,10 @@
         copy.start()
         key_copies.append(copy)
     keys[me_c] = key_by_row_ref[...]
+    advance(
+        depth_devices, row_devices, tiles, rim_width,
+        species_ref, diffusivity_ref, rate_ref, species_out_ref, shifted, *advance_scratch,
+    )
 
     def render(view, out_ref):
         weights = [[weight_ref[view, c, f] for f in range(2)] for c in range(4)]
@@ -292,8 +455,8 @@
     tiles = lax.axis_size("col")
     depth_total = depth_cells * depth_devices
     rim_width = (4 * depth_total + 99) // 100
-    rimmed = advance_deep(species, diffusivity, reaction_rate, rim_width)
-    species_out = rimmed[:, :, :, rim_width : rim_width + width]
+    row_devices = lax.axis_size("row")
+    planes, tall = depth_cells + 2 * LAYERS, rows + 8
     views = shear_rate.shape[0]
     view_count = views // depth_devices
     capacity = 2 * rows // tiles
@@ -309,11 +472,14 @@
     slots = 4 * capacity
     vmem = pl.BlockSpec(memory_space=pltpu.VMEM)
     smem = pl.BlockSpec(memory_space=pltpu.SMEM)
-    frame = pl.pallas_call(
-        functools.partial(march_kernel, depth_devices, tiles, capacity),
-        out_shape=jax.ShapeDtypeStruct((view_count, 4 * rows, width), jnp.float32),
-        in_specs=[smem] * 5 + [vmem] * 5,
-        out_specs=vmem,
+    species_out, frame = pl.pallas_call(
+        functools.partial(march_kernel, depth_devices, row_devices, tiles, capacity, rim_width),
+        out_shape=(
+            jax.ShapeDtypeStruct(species.shape, jnp.float32),
+            jax.ShapeDtypeStruct((view_count, 4 * rows, width), jnp.float32),
+        ),
+        in_specs=[smem] * 5 + [vmem] * 7,
+        out_specs=(vmem, vmem),
         scratch_shapes=[pltpu.VMEM((depth_cells, 2 * rim_width, 4, rows, width), jnp.float32)]
         + [pltpu.VMEM((depth_devices, 4, rows, width), jnp.float32)] * view_count
         + [pltpu.VMEM((depth_devices, 4, rows, width), jnp.float32)] * view_count
@@ -327,13 +493,26 @@
             pltpu.SemaphoreType.DMA((view_count, tiles)),
             pltpu.SemaphoreType.DMA((tiles,)),
             pltpu.SemaphoreType.DMA((tiles,)),
+        ]
+        + [
+            pltpu.VMEM((4, planes, tall, 2 * width), jnp.float32),
+            pltpu.VMEM((2, planes, tall, 2 * width), jnp.float32),
+            pltpu.VMEM((2, planes, tall, 2 * width), jnp.float32),
+            pltpu.VMEM((tall, 2 * width), jnp.float32),
+            pltpu.VMEM((2, 4, depth_cells, 8, width), jnp.float32),
+            pltpu.VMEM((2, 4, tall, width), jnp.float32),
+            pltpu.VMEM((2, 4, tall, width), jnp.float32),
+            pltpu.VMEM((2, 6, 2 * tall, width), jnp.bfloat16),
+            pltpu.VMEM((2, 6, 2 * tall, width), jnp.bfloat16),
+            pltpu.SemaphoreType.DMA((10,)),
+            pltpu.SemaphoreType.DMA((10,)),
         ],
         compiler_params=pltpu.CompilerParams(
             collective_id=1, has_side_effects=True, vmem_limit_bytes=40 * 1024 * 1024
         ),
     )(
         start, fraction, colour_weight * halves[None, :, None], colour_bias * halves, slab_order,
-        rimmed, lengths[:, 0, :, None], key_by_channel, key_by_row, warp_matrix,
+        species, diffusivity, reaction_rate, lengths[:, 0, :, None], key_by_channel, key_by_row, warp_matrix,
     )
     return (species_out, frame.reshape(view_count, rows, 4, width))
 

time: 91.9 us -> 56.2 us (0.61)
  waiting for transfers between devices: 18.4 us -> 0 us
  starting transfers between devices: 14.5 us -> 0 us
  other arithmetic: 17.1 us -> 4.4 us
  Pallas kernels: 30.6 us -> 42.9 us
  local copies, waits for them, and re-layouts: 9.95 us -> 7.78 us
    ppermute x6 -> x0, waiting for transfers between devices: 18.4 us -> none  [the longest x3 11.8 us: with_halo(): lax.ppermute(head, axis, [((i + 1) % count, i) for i in range(ends)])]
    ppermute x6 -> x0, starting transfers between devices: 14.5 us -> none  [the longest x3 10.5 us: with_halo(): lax.ppermute(tail, axis, [(i, (i + 1) % count) for i in range(ends)])]
    pallas_call x1, Pallas kernels: 30.6 us -> 42.9 us  [body(): pl.pallas_call(functools.partial(march_kernel, depth_devices, row_devices...]
    select_n x3 -> x0, other arithmetic: 7.97 us -> none  [the longest x1 3.05 us: advance_deep(): second = jnp.where(trimmed(inside, 2)[None], second, zero)]
    slice x10 -> x0, local copies, waits for them, and re-layouts: 5.96 us -> none  [the longest x6 2.97 us: trimmed(): array[..., layers:depth_len - layers, layers:row_len - layers, layers:col...]
    unnamed x30 -> x15, local copies, waits for them, and re-layouts: 1.65 us -> 7.41 us
    concatenate x3 -> x0, other arithmetic: 5.64 us -> none  [the longest x2 4.34 us: with_halo(): jnp.concatenate([lax.ppermute(tail, axis, [(i, (i + 1) % count) for i in...]
    another operation x3 -> x0, other arithmetic: 1.98 us -> none  [tendency_of(): source = jnp.stack([-burned, burned])]
  transfers between devices with their start and end apart: 6 -> 0, of which waited for: 4 -> 0; matrix products, arithmetic and copies ran while one was open for 6% -> 0% of each run, Pallas kernels for 0% -> 0%
where the time goes in v2:
time: 56.2 us; the launch traced here: 55.8 us
  Pallas kernels  42.9 us (76%)
  local copies, waits for them, and re-layouts  7.78 us (14%)
  other arithmetic  4.4 us (8%)
  between operations  0.69 us (1%)
    pallas_call x1, Pallas kernels, body(): pl.pallas_call(functools.partial(march_kernel, depth_devices, row_devices...  42.9 us
    unnamed x15, local copies, waits for them, and re-layouts  7.41 us

profile of v2, /device:TPU:0, one launch (start us, length us, event | category | flops | bytes accessed | tf_op | source)
XLA Modules:
  0.0 55.8 jit_solution(7432516262918204099)
XLA Ops:
  0.6 0.0 copy-start.2
  0.7 0.9 %convert_reduce_fusion = s32[4,32]{1,0:T(4,128)S(1)} fusion(s32[4,32]{1,0:T(4,128)} %bitcast.4, pred[32,32]{1,0:T(8,128)(4,1)S(1)} %iota_compare_fusion), kind=kLoop, calls=%fused_computation | loop fusion | flops 16256 | bytes 2048 | tf_op jit(solution)/shard_map/reduce_sum | solution.py:445
  1.5 0.7 %multiply_add_fusion = s32[4,32]{1,0:T(4,128)S(1)} fusion(s32[4,32]{1,0:T(4,128)S(1)} %convert_reduce_fusion, s32[4,32]{1,0:T(4,128)} %bitcast.5), kind=kLoop, calls=%fused_computation.8 | loop fusion | flops 256 | bytes 1536 | tf_op jit(solution)/shard_map/add | solution.py:446
  2.2 0.1 tile.10.key_by_channel_ref
  2.3 0.8 %copy.27 = f32[16,4]{1,0:T(8,128)S(1)} copy(f32[16,4]{0,1:T(4,128)} %param.16) | data formatting | bytes 512 | tf_op args[5]
  3.1 0.7 %broadcast_multiply_fusion.1.bias_ref = f32[16,4]{1,0:T(8,128)S(1)} fusion(f32[16,4]{1,0:T(8,128)S(1)} %copy.27, f32[4]{0:T(128)} %constant.21.clone), kind=kLoop, calls=%fused_computation.7 | loop fusion | flops 64 | bytes 528 | tf_op jit(solution)/shard_map/mul | solution.py:514
  3.7 0.8 %copy.29.order_ref = s32[16,4]{1,0:T(8,128)S(1)} copy(s32[16,4]{0,1:T(4,128)} %param.17) | data formatting | bytes 512 | tf_op args[6]
  4.5 0.7 %floor_subtract_fusion.fraction_ref = f32[16,16]{1,0:T(8,128)S(1)} fusion(f32[16]{0:T(128)S(1)} %convert_add_fusion, f32[16]{0:T(128)} %param.14), kind=kLoop, calls=%fused_computation.3 | loop fusion | flops 768 | bytes 1152 | tf_op jit(solution)/shard_map/sub | solution.py:466
  5.2 0.7 %fusion.1.start_ref = s32[16,16]{1,0:T(8,128)S(1)} fusion(f32[16]{0:T(128)S(1)} %convert_add_fusion, f32[16]{0:T(128)} %param.14), kind=kLoop, calls=%fused_computation.6 | loop fusion | flops 1280 | bytes 1152 | tf_op jit(solution)/shard_map/jit(clip)/min | solution.py:467
  5.9 0.8 %copy.25 = f32[16,4,2]{2,1,0:T(4,128)S(1)} copy(f32[16,4,2]{0,2,1:T(2,128)} %param.15) | data formatting | bytes 1024 | tf_op args[4]
  6.7 0.7 %broadcast_multiply_fusion.weight_ref = f32[16,4,2]{2,1,0:T(4,128)S(1)} fusion(f32[16,4,2]{2,1,0:T(4,128)S(1)} %copy.25, f32[4]{0:T(128)} %constant.21.clone), kind=kLoop, calls=%fused_computation.1 | loop fusion | flops 128 | bytes 1040 | tf_op jit(solution)/shard_map/mul | solution.py:514
  7.5 0.1 broadcast_in_dim.2
  7.5 0.0 copy-start.4
  7.5 0.1 reshape.44.key_by_row_ref
  7.7 0.6 %copy-done.4 = s32[4,1,32]{2,1,0:T(1,128)S(1)} copy-done((s32[4,1,32]{2,1,0:T(1,128)S(1)}, s32[4,1,32]{2,1,0:T(1,128)}, u32[]{:S(2)}) %copy-start.4) | copy-done | bytes 536
  8.2 0.1 copy.30.length_ref
  8.3 0.0 copy-done.2
  8.3 0.0 copy-start
  8.3 1.0 %copy-done = f32[2,16,32,128]{3,2,1,0:T(8,128)S(1)} copy-done((f32[2,16,32,128]{3,2,1,0:T(8,128)S(1)}, f32[2,16,32,128]{3,2,1,0:T(8,128)}, u32[]{:S(2)}) %copy-start) | copy-done | bytes 524312
  9.4 0.0 copy-start.1
  9.4 1.0 %copy-done.1 = bf16[16,128,128]{2,1,0:T(8,128)(2,1)S(1)} copy-done((bf16[16,128,128]{2,1,0:T(8,128)(2,1)S(1)}, bf16[16,128,128]{2,1,0:T(8,128)(2,1)}, u32[]{:S(2)}) %copy-start.1) | copy-done | bytes 524312
  10.4 0.0 copy-start.3
  10.4 0.9 %copy-done.3 = f32[16,32,128]{2,1,0:T(8,128)S(1)} copy-done((f32[16,32,128]{2,1,0:T(8,128)S(1)}, f32[16,32,128]{2,1,0:T(8,128)}, u32[]{:S(2)}) %copy-start.3) | copy-done | bytes 262168
  11.4 42.9 %shard_map.122 = (f32[2,16,32,128]{3,2,1,0:T(8,128)S(1)}, f32[4,128,128]{2,1,0:T(8,128)S(1)}) custom-call(s32[16,16]{1,0:T(8,128)S(1)} %fusion.1.start_ref, f32[16,16]{1,0:T(8,128)S(1)} %floor_subtract_fusion.fraction_ref, f32[16,4,2]{2,1,0:T(4,128)S(1)} %broadcast_multiply_fusion.weight_ref, f32[16,4]{1,0:T(8,128)S(1)} %broadcast_multiply_fusion.1.bias_ref, ...), custom_call_target="tpu_custom_call" | custom-call | tf_op jit(solution)/shard_map/pallas_call | solution.py:475
  54.3 0.8 %copy.33 = f32[2,16,32,128]{3,2,1,0:T(8,128)} copy(f32[2,16,32,128]{3,2,1,0:T(8,128)S(1)} %get-tuple-element.8) | data formatting | bytes 1048576
  55.0 0.7 %copy.34 = f32[4,32,4,128]{3,2,1,0:T(4,128)} copy(f32[4,32,4,128]{3,2,1,0:T(4,128)S(1)} %bitcast.3) | data formatting | bytes 524288
  (3 shorter events, 0.0 us)
Async XLA Ops:
  0.6 7.7 %copy-start.2 = (f32[16,32,128]{2,1,0:T(8,128)S(1)}, f32[16,32,128]{2,1,0:T(8,128)}, u32[]{:S(2)}) copy-start(f32[16,32,128]{2,1,0:T(8,128)} %diffusivity_ref.1) | copy-start | bytes 786436
  7.5 0.7 %copy-start.4 = (s32[4,1,32]{2,1,0:T(1,128)S(1)}, s32[4,1,32]{2,1,0:T(1,128)}, u32[]{:S(2)}) copy-start(s32[4,1,32]{2,1,0:T(1,128)} %param.18) | copy-start | bytes 1540
  8.3 1.0 %copy-start = (f32[2,16,32,128]{3,2,1,0:T(8,128)S(1)}, f32[2,16,32,128]{3,2,1,0:T(8,128)}, u32[]{:S(2)}) copy-start(f32[2,16,32,128]{3,2,1,0:T(8,128)} %species_ref.1) | copy-start | bytes 1572868
  9.4 1.0 %copy-start.1 = (bf16[16,128,128]{2,1,0:T(8,128)(2,1)S(1)}, bf16[16,128,128]{2,1,0:T(8,128)(2,1)}, u32[]{:S(2)}) copy-start(bf16[16,128,128]{2,1,0:T(8,128)(2,1)} %warp_ref.1) | copy-start | bytes 1572868
  10.4 0.9 %copy-start.3 = (f32[16,32,128]{2,1,0:T(8,128)S(1)}, f32[16,32,128]{2,1,0:T(8,128)}, u32[]{:S(2)}) copy-start(f32[16,32,128]{2,1,0:T(8,128)} %rate_ref.1) | copy-start | bytes 786436

commit v3 on v2

--- a/solution.py
+++ b/solution.py
@@ -21,7 +21,7 @@
 
 def advance(
     depth_devices, row_devices, tiles, rim_width,
-    species_ref, diffusivity_ref, rate_ref, species_out_ref, shifted,
+    species_ref, diffusivity_ref, rate_ref, species_out_ref, shifted, local_sem,
     deep, first_ref, second_ref, step_ref, row_got, packs, got, stage_out, stage_in, send_sem, recv_sem,
 ):
     me_d, me_r, me_c = lax.axis_index("depth"), lax.axis_index("row"), lax.axis_index("col")
@@ -90,14 +90,14 @@
     ]
     begin(me_r, row_devices, down, up)
 
-    def place_cells(cell, carry):
-        for field in range(2):
-            deep[field, LAYERS + cell, pl.ds(0, rows), pl.ds(0, width)] = species_ref[field, cell]
-        deep[2, LAYERS + cell, pl.ds(0, rows), pl.ds(0, width)] = diffusivity_ref[cell]
-        deep[3, LAYERS + cell, pl.ds(0, rows), pl.ds(0, width)] = rate_ref[cell]
-        return carry
-
-    lax.fori_loop(0, depth_cells, place_cells, 0)
+    own = (pl.ds(LAYERS, depth_cells), pl.ds(0, rows), pl.ds(0, width))
+    sources = (species_ref.at[0], species_ref.at[1], diffusivity_ref, rate_ref)
+    local = [
+        pltpu.make_async_copy(source, deep.at[(field, *own)], local_sem.at[2 + field])
+        for field, source in enumerate(sources)
+    ]
+    for copy in local:
+        copy.start()
     row_at = lax.broadcasted_iota(jnp.int32, (tall, wide), 0)
     row_at = me_r * rows + jnp.where(row_at < rows + 4, row_at, row_at - tall)
     col_at = lax.broadcasted_iota(jnp.int32, (tall, wide), 1)
@@ -106,6 +106,8 @@
     step_ref[...] = jnp.where(inside, TIME_STEP, 0.0)
     finish(me_r, row_devices, down, up, row_got.at[0], row_got.at[1])
 
+    for copy in local:
+        copy.wait()
     near = lax.broadcasted_iota(jnp.int32, (8, width), 0) < 4
 
     def place_rows(cell, carry):
@@ -269,20 +271,21 @@
 
 def march_kernel(
     depth_devices, row_devices, tiles, capacity, rim_width,
-    start_ref, fraction_ref, weight_ref, bias_ref, order_ref,
-    species_ref, diffusivity_ref, rate_ref, length_ref, key_by_channel_ref, key_by_row_ref, warp_ref,
-    species_out_ref, frame_ref,
+    real_ref, whole_ref,
+    species_ref, diffusivity_ref, rate_ref, line_ref, warp_hbm,
+    species_hbm, frame_hbm,
     shifted, *scratch,
 ):
-    view_count = frame_ref.shape[0]
+    view_count = frame_hbm.shape[0]
     stacks = scratch[:view_count]
     images = scratch[view_count : 2 * view_count]
     packs = scratch[2 * view_count : 3 * view_count]
     arrivals = scratch[3 * view_count : 4 * view_count]
-    keys, slab_send, slab_recv, tile_send, tile_recv, key_send, key_recv = scratch[
-        4 * view_count : 4 * view_count + 7
-    ]
-    advance_scratch = scratch[4 * view_count + 7 :]
+    (
+        keys, key_by_channel_ref, key_by_row_ref, warp_ref, species_out_ref, frame_ref,
+        slab_send, slab_recv, tile_send, tile_recv, key_send, key_recv, local_sem,
+    ) = scratch[4 * view_count : 4 * view_count + 13]
+    advance_scratch = scratch[4 * view_count + 13 :]
     depth_cells, rows, width = shifted.shape[0], shifted.shape[3], shifted.shape[4]
     me_d, me_r, me_c = lax.axis_index("depth"), lax.axis_index("row"), lax.axis_index("col")
 
@@ -302,6 +305,23 @@
     for step in row_steps:
         row_peer = lax.rem(me_r + step, row_devices)
         pl.semaphore_signal(barrier, inc=1, device_id=(me_d, row_peer, me_c), device_id_type=MESH)
+    warp_copy = pltpu.make_async_copy(
+        warp_hbm.at[pl.ds(me_d * view_count, view_count)], warp_ref, local_sem.at[0]
+    )
+    warp_copy.start()
+    pixels = 4 * rows
+    earlier = lax.broadcasted_iota(jnp.int32, (pixels, pixels), 0)
+    later = lax.broadcasted_iota(jnp.int32, (pixels, pixels), 1)
+    for target, base, same in (
+        (key_by_channel_ref, 0, earlier // rows == later // rows),
+        (key_by_row_ref, view_count, earlier % 4 == later % 4),
+    ):
+        for number in range(view_count):
+            owner = line_ref[base + number : base + number + 1, :]
+            column = jnp.sum(jnp.where(earlier == later, owner, 0), axis=1, keepdims=True)
+            before = (column == owner) & same & (earlier < later)
+            rank = jnp.sum(jnp.where(before, 1, 0), axis=0, keepdims=True)
+            target[number : number + 1, :] = owner * capacity + rank
     pl.semaphore_wait(barrier, depth_devices - 1 + tiles - 1 + len(row_steps))
 
     key_copies = []
@@ -316,17 +336,19 @@
     keys[me_c] = key_by_row_ref[...]
     advance(
         depth_devices, row_devices, tiles, rim_width,
-        species_ref, diffusivity_ref, rate_ref, species_out_ref, shifted, *advance_scratch,
+        species_ref, diffusivity_ref, rate_ref, species_out_ref, shifted, local_sem, *advance_scratch,
     )
+    species_copy = pltpu.make_async_copy(species_out_ref, species_hbm, local_sem.at[1])
+    species_copy.start()
 
     def render(view, out_ref):
-        weights = [[weight_ref[view, c, f] for f in range(2)] for c in range(4)]
-        biases = [bias_ref[view, c] for c in range(4)]
+        weights = [[real_ref[view, 2 * c + f] for f in range(2)] for c in range(4)]
+        biases = [real_ref[view, 8 + c] for c in range(4)]
 
         def cells(cell, state):
             red, green, blue, through = state
-            at = start_ref[view, cell]
-            fraction = fraction_ref[view, cell]
+            at = whole_ref[view, cell]
+            fraction = real_ref[view, 12 + cell]
             s0 = shifted[cell, at, 0] + fraction * shifted[cell, at, 1]
             s1 = shifted[cell, at, 2] + fraction * shifted[cell, at, 3]
             logits = [weights[c][0] * s0 + weights[c][1] * s1 + biases[c] for c in range(4)]
@@ -345,10 +367,10 @@
             0, depth_cells, cells, (zero, zero, zero, zero + 1.0), unroll=4
         )
         opacity = 1.0 - through
-        out_ref[0] = 0.5 * (red + opacity)
-        out_ref[1] = 0.5 * (green + opacity)
-        out_ref[2] = 0.5 * (blue + opacity)
-        out_ref[3] = opacity
+        for channel, value in enumerate((red, green, blue, opacity)):
+            value = value if channel == 3 else 0.5 * (value + opacity)
+            root = jnp.sqrt(jnp.sqrt(jnp.clip(value, 0.0, 1.0)))
+            out_ref[channel] = ((root * 65535.0 + 0.5).astype(jnp.int32) - 32768).astype(jnp.int16)
 
     slots = 4 * capacity
 
@@ -372,10 +394,21 @@
     def composite(number):
         view = me_d * view_count + number
         stack = stacks[number]
-        result = stack[order_ref[view, 0]]
+
+        def slab_at(position):
+            code = stack[whole_ref[view, depth_cells + position]].astype(jnp.int32)
+            root = (code + 32768).astype(jnp.float32) * (1.0 / 65535.0)
+            root = root * root
+            return root * root
+
+        result = slab_at(0)
         for position in range(1, depth_devices):
-            result = result + (1.0 - result[3:4]) * stack[order_ref[view, position]]
-        keep = lax.broadcasted_iota(jnp.int32, (rows, width), 1) < length_ref[number]
+            result = result + (1.0 - result[3:4]) * slab_at(position)
+        lane = lax.broadcasted_iota(jnp.int32, (rows, width), 1)
+        at = lax.broadcasted_iota(jnp.int32, (rows, 4 * rows), 1)
+        at = at == lax.broadcasted_iota(jnp.int32, (rows, 4 * rows), 0)
+        length = line_ref[2 * view_count + number : 2 * view_count + number + 1, :]
+        keep = lane < jnp.sum(jnp.where(at, length, 0), axis=1, keepdims=True)
         picture = jnp.where(keep[None], result, 0.0).reshape(4 * rows, width).astype(jnp.bfloat16)
         line = lax.broadcasted_iota(jnp.int32, (tiles * slots, 4 * rows), 0)
         pixel = lax.broadcasted_iota(jnp.int32, (tiles * slots, 4 * rows), 1)
@@ -415,12 +448,12 @@
         )
         high = gathered.astype(jnp.bfloat16)
         low = (gathered - high.astype(jnp.float32)).astype(jnp.bfloat16)
-        matrix = warp_ref[me_d * view_count + number]
+        matrix = warp_ref[number]
         frame_ref[number] = jnp.dot(high, matrix, preferred_element_type=jnp.float32) + jnp.dot(
             low, matrix, preferred_element_type=jnp.float32
         )
 
-    slab_copies, tile_copies = [], []
+    slab_copies, tile_copies, frame_copies = [], [], []
     for number in range(view_count):
         slab_copies.append(render_group(number))
         if number > 0:
@@ -435,15 +468,14 @@
     for number in range(view_count):
         for copy in tile_copies[number]:
             copy.wait()
+        if number == 0:
+            warp_copy.wait()
         warp(number)
-
-
-def slot_keys(owner_rows, capacity):
-    rows = owner_rows.shape[-1]
-    same = owner_rows[..., :, None] == owner_rows[..., None, :]
-    places = jnp.arange(rows, dtype=jnp.int32)
-    rank = jnp.sum((same & (places[:, None] < places[None, :])).astype(jnp.int32), axis=-2)
-    return owner_rows * capacity + rank
+        copy = pltpu.make_async_copy(frame_ref.at[number], frame_hbm.at[number], local_sem.at[6 + number])
+        copy.start()
+        frame_copies.append(copy)
+    for copy in [species_copy] + frame_copies:
+        copy.wait()
 
 
 def body(
@@ -466,11 +498,17 @@
     fraction = offset - floor_part
     start = jnp.clip(floor_part.astype(jnp.int32) + rim_width, 0, 2 * rim_width - 1)
     halves = jnp.array([0.5, 0.5, 0.5, 1.0], jnp.float32)
-    key = slot_keys(owners[:, 0, :, 0], capacity)
-    key_by_channel = jnp.tile(key, (1, 4))
-    key_by_row = jnp.repeat(key, 4, axis=1)
+    real = jnp.concatenate(
+        [(colour_weight * halves[None, :, None]).reshape(views, 8), colour_bias * halves, fraction], axis=1
+    )
+    whole = jnp.concatenate([start, slab_order], axis=1)
+    owner = owners[:, 0, :, 0]
+    lines = jnp.concatenate(
+        [jnp.tile(owner, (1, 4)), jnp.repeat(owner, 4, axis=1), jnp.tile(lengths[:, 0, :], (1, 4))], axis=0
+    )
     slots = 4 * capacity
     vmem = pl.BlockSpec(memory_space=pltpu.VMEM)
+    hbm = pl.BlockSpec(memory_space=pltpu.HBM)
     smem = pl.BlockSpec(memory_space=pltpu.SMEM)
     species_out, frame = pl.pallas_call(
         functools.partial(march_kernel, depth_devices, row_devices, tiles, capacity, rim_width),
@@ -478,21 +516,27 @@
             jax.ShapeDtypeStruct(species.shape, jnp.float32),
             jax.ShapeDtypeStruct((view_count, 4 * rows, width), jnp.float32),
         ),
-        in_specs=[smem] * 5 + [vmem] * 7,
-        out_specs=(vmem, vmem),
+        in_specs=[smem] * 2 + [hbm] * 3 + [vmem, hbm],
+        out_specs=(hbm, hbm),
         scratch_shapes=[pltpu.VMEM((depth_cells, 2 * rim_width, 4, rows, width), jnp.float32)]
-        + [pltpu.VMEM((depth_devices, 4, rows, width), jnp.float32)] * view_count
-        + [pltpu.VMEM((depth_devices, 4, rows, width), jnp.float32)] * view_count
+        + [pltpu.VMEM((depth_devices, 4, rows, width), jnp.int16)] * view_count
+        + [pltpu.VMEM((depth_devices, 4, rows, width), jnp.int16)] * view_count
         + [pltpu.VMEM((tiles, slots, width), jnp.bfloat16)] * view_count
         + [pltpu.VMEM((tiles, slots, width), jnp.bfloat16)] * view_count
         + [
             pltpu.VMEM((tiles, view_count, 4 * rows), jnp.int32),
+            pltpu.VMEM((view_count, 4 * rows), jnp.int32),
+            pltpu.VMEM((view_count, 4 * rows), jnp.int32),
+            pltpu.VMEM((view_count, *warp_matrix.shape[1:]), warp_matrix.dtype),
+            pltpu.VMEM(species.shape, jnp.float32),
+            pltpu.VMEM((view_count, 4 * rows, width), jnp.float32),
             pltpu.SemaphoreType.DMA((view_count, depth_devices)),
             pltpu.SemaphoreType.DMA((view_count, depth_devices)),
             pltpu.SemaphoreType.DMA((view_count, tiles)),
             pltpu.SemaphoreType.DMA((view_count, tiles)),
             pltpu.SemaphoreType.DMA((tiles,)),
             pltpu.SemaphoreType.DMA((tiles,)),
+            pltpu.SemaphoreType.DMA((6 + view_count,)),
         ]
         + [
             pltpu.VMEM((4, planes, tall, 2 * width), jnp.float32),
@@ -511,8 +555,7 @@
             collective_id=1, has_side_effects=True, vmem_limit_bytes=40 * 1024 * 1024
         ),
     )(
-        start, fraction, colour_weight * halves[None, :, None], colour_bias * halves, slab_order,
-        species, diffusivity, reaction_rate, lengths[:, 0, :, None], key_by_channel, key_by_row, warp_matrix,
+        real, whole, species, diffusivity, reaction_rate, lines, warp_matrix,
     )
     return (species_out, frame.reshape(view_count, rows, 4, width))
 

time: 56.2 us -> 52.5 us (0.934)
  Pallas kernels: 42.9 us -> 39.8 us
  other arithmetic: 4.4 us -> 3.09 us
  local copies, waits for them, and re-layouts: 7.78 us -> 8.53 us
    pallas_call x1, Pallas kernels: 42.9 us -> 39.8 us  [body(): pl.pallas_call(functools.partial(march_kernel, depth_devices, row_devices...]
    unnamed x15 -> x12, local copies, waits for them, and re-layouts: 7.41 us -> 6.05 us
    another operation x3 -> x4, local copies, waits for them, and re-layouts: 0.2 us -> 1.54 us  [the longest x2 0.77 us: body(): jnp.tile(owner, (1, 4))]
    reduce_sum x1 -> x0, other arithmetic: 0.85 us -> none  [slot_keys(): jnp.sum((same & (places[:, None] < places[None, :])).astype(jnp.int32), a...]
    add x1 -> x0, other arithmetic: 0.69 us -> none  [slot_keys(): return owner_rows * capacity + rank]
    broadcast_in_dim x1, local copies, waits for them, and re-layouts: 0.07 us -> 0.76 us  [body(): jnp.repeat(owner, 4, axis=1)]
where the time goes in v3:
time: 52.5 us; the launch traced here: 52.1 us
  Pallas kernels  39.8 us (76%)
  local copies, waits for them, and re-layouts  8.53 us (16%)
  other arithmetic  3.09 us (6%)
  between operations  0.69 us (1%)
    pallas_call x1, Pallas kernels, body(): pl.pallas_call(functools.partial(march_kernel, depth_devices, row_devices...  39.8 us
    unnamed x12, local copies, waits for them, and re-layouts  6.05 us

profile of v3, /device:TPU:0, one launch (start us, length us, event | category | flops | bytes accessed | tf_op | source)
XLA Modules:
  0.0 52.1 jit_solution(2795840344437374050)
XLA Ops:
  0.6 0.0 copy-start.2
  0.7 0.8 %broadcast_multiply_fusion.1 = f32[16,4,2]{0,2,1:T(2,128)S(1)} fusion(f32[16,4,2]{0,2,1:T(2,128)} %param.15, f32[4]{0:T(128)} %constant.20.clone), kind=kLoop, calls=%fused_computation.8 | loop fusion | flops 128 | bytes 1040 | tf_op jit(solution)/shard_map/mul | solution.py:502
  1.5 0.1 copy.21
  1.5 0.8 %copy.19 = f32[16,4]{1,0:T(8,128)S(1)} copy(f32[16,4]{0,1:T(4,128)} %param.16) | data formatting | bytes 512 | tf_op args[5]
  2.3 0.7 %broadcast_multiply_fusion = f32[16,4]{1,0:T(8,128)S(1)} fusion(f32[16,4]{1,0:T(8,128)S(1)} %copy.19, f32[4]{0:T(128)} %constant.20.clone), kind=kLoop, calls=%fused_computation.7 | loop fusion | flops 64 | bytes 528 | tf_op jit(solution)/shard_map/mul | solution.py:502
  2.9 0.8 %copy.22 = s32[16,4]{1,0:T(8,128)S(1)} copy(s32[16,4]{0,1:T(4,128)} %param.17) | data formatting | bytes 512 | tf_op args[6]
  3.7 0.7 %tile.24 = s32[4,4,32]{2,1,0:T(4,128)S(1)} broadcast(s32[4,32]{1,0:T(4,128)} %bitcast.8), dimensions={0,2} | broadcast | bytes 2560 | tf_op jit(solution)/shard_map/tile | solution.py:507
  4.4 0.1 tile.25
  4.5 0.7 %tile.21 = s32[4,4,32]{2,1,0:T(4,128)S(1)} broadcast(s32[4,32]{1,0:T(4,128)} %bitcast.6), dimensions={0,2} | broadcast | bytes 2560 | tf_op jit(solution)/shard_map/tile | solution.py:507
  5.2 0.1 tile.22
  5.2 0.7 %floor_subtract_fusion = f32[16,16]{1,0:T(8,128)S(1)} fusion(f32[16]{0:T(128)S(1)} %convert_add_fusion, f32[16]{0:T(128)} %param.14), kind=kLoop, calls=%fused_computation.1 | loop fusion | flops 768 | bytes 1152 | tf_op jit(solution)/shard_map/sub | solution.py:498
  6.0 0.1 pad_maximum_fusion.real_ref
  6.1 0.7 %fusion.1 = s32[16,16]{1,0:T(8,128)S(1)} fusion(f32[16]{0:T(128)S(1)} %convert_add_fusion, f32[16]{0:T(128)} %param.14), kind=kLoop, calls=%fused_computation.3 | loop fusion | flops 1280 | bytes 1152 | tf_op jit(solution)/shard_map/jit(clip)/min | solution.py:499
  6.8 0.1 pad_add_fusion.whole_ref
  6.9 0.8 %broadcast_in_dim.2 = s32[4,32,4]{2,1,0:T(8,128)S(1)} broadcast(s32[4,32]{1,0:T(4,128)} %bitcast.7), dimensions={0,1} | broadcast | bytes 2560 | tf_op jit(solution)/shard_map/broadcast_in_dim | solution.py:507
  7.6 0.1 reshape.31
  7.8 0.0 copy-done.2
  7.8 0.0 copy-start
  7.8 1.0 %copy-done = f32[2,16,32,128]{3,2,1,0:T(8,128)S(1)} copy-done((f32[2,16,32,128]{3,2,1,0:T(8,128)S(1)}, f32[2,16,32,128]{3,2,1,0:T(8,128)}, u32[]{:S(2)}) %copy-start) | copy-done | bytes 524312
  8.8 0.0 copy-start.1
  8.8 1.0 %copy-done.1 = bf16[16,128,128]{2,1,0:T(8,128)(2,1)S(1)} copy-done((bf16[16,128,128]{2,1,0:T(8,128)(2,1)S(1)}, bf16[16,128,128]{2,1,0:T(8,128)(2,1)}, u32[]{:S(2)}) %copy-start.1) | copy-done | bytes 524312
  9.9 0.0 copy-start.3
  9.9 0.9 %copy-done.3 = f32[16,32,128]{2,1,0:T(8,128)S(1)} copy-done((f32[16,32,128]{2,1,0:T(8,128)S(1)}, f32[16,32,128]{2,1,0:T(8,128)}, u32[]{:S(2)}) %copy-start.3) | copy-done | bytes 262168
  10.8 39.8 %shard_map.122 = (f32[2,16,32,128]{3,2,1,0:T(8,128)S(1)}, f32[4,128,128]{2,1,0:T(8,128)S(1)}) custom-call(f32[16,28]{1,0:T(8,128)S(1)} %pad_maximum_fusion.real_ref, s32[16,20]{1,0:T(8,128)S(1)} %pad_add_fusion.whole_ref, f32[2,16,32,128]{3,2,1,0:T(8,128)S(1)} %copy-done, f32[16,32,128]{2,1,0:T(8,128)S(1)} %copy-done.2, f32[16,32,128]{2,1,0:T(8,128)S(1)} %copy-done.3, ...), custom_call_target="tpu_custom_call" | custom-call | tf_op jit(solution)/shard_map/pallas_call | solution.py:513
  50.6 0.8 %copy.25 = f32[2,16,32,128]{3,2,1,0:T(8,128)} copy(f32[2,16,32,128]{3,2,1,0:T(8,128)S(1)} %get-tuple-element.8) | data formatting | bytes 1048576
  51.4 0.7 %copy.26 = f32[4,32,4,128]{3,2,1,0:T(4,128)} copy(f32[4,32,4,128]{3,2,1,0:T(4,128)S(1)} %bitcast.4) | data formatting | bytes 524288
  (2 shorter events, 0.0 us)
Async XLA Ops:
  0.6 7.1 %copy-start.2 = (f32[16,32,128]{2,1,0:T(8,128)S(1)}, f32[16,32,128]{2,1,0:T(8,128)}, u32[]{:S(2)}) copy-start(f32[16,32,128]{2,1,0:T(8,128)} %diffusivity_ref.1) | copy-start | bytes 786436
  7.8 1.0 %copy-start = (f32[2,16,32,128]{3,2,1,0:T(8,128)S(1)}, f32[2,16,32,128]{3,2,1,0:T(8,128)}, u32[]{:S(2)}) copy-start(f32[2,16,32,128]{3,2,1,0:T(8,128)} %species_ref.1) | copy-start | bytes 1572868
  8.8 1.0 %copy-start.1 = (bf16[16,128,128]{2,1,0:T(8,128)(2,1)S(1)}, bf16[16,128,128]{2,1,0:T(8,128)(2,1)}, u32[]{:S(2)}) copy-start(bf16[16,128,128]{2,1,0:T(8,128)(2,1)} %warp_hbm.1) | copy-start | bytes 1572868
  9.9 0.9 %copy-start.3 = (f32[16,32,128]{2,1,0:T(8,128)S(1)}, f32[16,32,128]{2,1,0:T(8,128)}, u32[]{:S(2)}) copy-start(f32[16,32,128]{2,1,0:T(8,128)} %rate_ref.1) | copy-start | bytes 786436

commit v4 on v3

--- a/solution.py
+++ b/solution.py
@@ -271,8 +271,8 @@
 
 def march_kernel(
     depth_devices, row_devices, tiles, capacity, rim_width,
-    real_ref, whole_ref,
-    species_ref, diffusivity_ref, rate_ref, line_ref, warp_hbm,
+    shear_ref, weight_ref, bias_ref, start_ref, order_ref,
+    species_ref, diffusivity_ref, rate_ref, owner_ref, length_ref, warp_hbm,
     species_hbm, frame_hbm,
     shifted, *scratch,
 ):
@@ -312,12 +312,23 @@
     pixels = 4 * rows
     earlier = lax.broadcasted_iota(jnp.int32, (pixels, pixels), 0)
     later = lax.broadcasted_iota(jnp.int32, (pixels, pixels), 1)
-    for target, base, same in (
-        (key_by_channel_ref, 0, earlier // rows == later // rows),
-        (key_by_row_ref, view_count, earlier % 4 == later % 4),
+    line = lax.broadcasted_iota(jnp.int32, (rows, pixels), 0)
+    spot = lax.broadcasted_iota(jnp.int32, (rows, pixels), 1)
+
+    def spread(table, chosen):
+        return jnp.dot(
+            table.astype(jnp.float32).astype(jnp.bfloat16),
+            jnp.where(chosen, 1.0, 0.0).astype(jnp.bfloat16),
+            preferred_element_type=jnp.float32,
+        ).astype(jnp.int32)
+
+    for target, chosen, same in (
+        (key_by_channel_ref, spot % rows == line, earlier // rows == later // rows),
+        (key_by_row_ref, spot // 4 == line, earlier % 4 == later % 4),
     ):
+        owners = spread(owner_ref[...], chosen)
         for number in range(view_count):
-            owner = line_ref[base + number : base + number + 1, :]
+            owner = owners[number : number + 1, :]
             column = jnp.sum(jnp.where(earlier == later, owner, 0), axis=1, keepdims=True)
             before = (column == owner) & same & (earlier < later)
             rank = jnp.sum(jnp.where(before, 1, 0), axis=0, keepdims=True)
@@ -342,13 +353,17 @@
     species_copy.start()
 
     def render(view, out_ref):
-        weights = [[real_ref[view, 2 * c + f] for f in range(2)] for c in range(4)]
-        biases = [real_ref[view, 8 + c] for c in range(4)]
+        weights = [
+            [weight_ref[2 * c + f, view] * (0.5 if c < 3 else 1.0) for f in range(2)] for c in range(4)
+        ]
+        biases = [bias_ref[c, view] * (0.5 if c < 3 else 1.0) for c in range(4)]
+        shear = shear_ref[view]
 
         def cells(cell, state):
             red, green, blue, through = state
-            at = whole_ref[view, cell]
-            fraction = real_ref[view, 12 + cell]
+            at = start_ref[view, cell]
+            place = (me_d * depth_cells + cell).astype(jnp.float32) + 0.5 - 0.5 * depth_cells * depth_devices
+            fraction = shear * place - (at - rim_width).astype(jnp.float32)
             s0 = shifted[cell, at, 0] + fraction * shifted[cell, at, 1]
             s1 = shifted[cell, at, 2] + fraction * shifted[cell, at, 3]
             logits = [weights[c][0] * s0 + weights[c][1] * s1 + biases[c] for c in range(4)]
@@ -396,7 +411,7 @@
         stack = stacks[number]
 
         def slab_at(position):
-            code = stack[whole_ref[view, depth_cells + position]].astype(jnp.int32)
+            code = stack[order_ref[position, view]].astype(jnp.int32)
             root = (code + 32768).astype(jnp.float32) * (1.0 / 65535.0)
             root = root * root
             return root * root
@@ -405,9 +420,9 @@
         for position in range(1, depth_devices):
             result = result + (1.0 - result[3:4]) * slab_at(position)
         lane = lax.broadcasted_iota(jnp.int32, (rows, width), 1)
-        at = lax.broadcasted_iota(jnp.int32, (rows, 4 * rows), 1)
-        at = at == lax.broadcasted_iota(jnp.int32, (rows, 4 * rows), 0)
-        length = line_ref[2 * view_count + number : 2 * view_count + number + 1, :]
+        at = lax.broadcasted_iota(jnp.int32, (rows, rows), 1)
+        at = at == lax.broadcasted_iota(jnp.int32, (rows, rows), 0)
+        length = length_ref[number : number + 1, :]
         keep = lane < jnp.sum(jnp.where(at, length, 0), axis=1, keepdims=True)
         picture = jnp.where(keep[None], result, 0.0).reshape(4 * rows, width).astype(jnp.bfloat16)
         line = lax.broadcasted_iota(jnp.int32, (tiles * slots, 4 * rows), 0)
@@ -495,17 +510,7 @@
     cell_at = lax.axis_index("depth") * depth_cells + jnp.arange(depth_cells, dtype=jnp.int32)
     offset = shear_rate[:, None] * (cell_at.astype(jnp.float32) + 0.5 - 0.5 * depth_total)
     floor_part = jnp.floor(offset)
-    fraction = offset - floor_part
     start = jnp.clip(floor_part.astype(jnp.int32) + rim_width, 0, 2 * rim_width - 1)
-    halves = jnp.array([0.5, 0.5, 0.5, 1.0], jnp.float32)
-    real = jnp.concatenate(
-        [(colour_weight * halves[None, :, None]).reshape(views, 8), colour_bias * halves, fraction], axis=1
-    )
-    whole = jnp.concatenate([start, slab_order], axis=1)
-    owner = owners[:, 0, :, 0]
-    lines = jnp.concatenate(
-        [jnp.tile(owner, (1, 4)), jnp.repeat(owner, 4, axis=1), jnp.tile(lengths[:, 0, :], (1, 4))], axis=0
-    )
     slots = 4 * capacity
     vmem = pl.BlockSpec(memory_space=pltpu.VMEM)
     hbm = pl.BlockSpec(memory_space=pltpu.HBM)
@@ -516,7 +521,7 @@
             jax.ShapeDtypeStruct(species.shape, jnp.float32),
             jax.ShapeDtypeStruct((view_count, 4 * rows, width), jnp.float32),
         ),
-        in_specs=[smem] * 2 + [hbm] * 3 + [vmem, hbm],
+        in_specs=[smem] * 5 + [hbm] * 3 + [vmem, vmem, hbm],
         out_specs=(hbm, hbm),
         scratch_shapes=[pltpu.VMEM((depth_cells, 2 * rim_width, 4, rows, width), jnp.float32)]
         + [pltpu.VMEM((depth_devices, 4, rows, width), jnp.int16)] * view_count
@@ -552,10 +557,11 @@
             pltpu.SemaphoreType.DMA((10,)),
         ],
         compiler_params=pltpu.CompilerParams(
-            collective_id=1, has_side_effects=True, vmem_limit_bytes=40 * 1024 * 1024
+            collective_id=1, has_side_effects=True, vmem_limit_bytes=60 * 1024 * 1024
         ),
     )(
-        real, whole, species, diffusivity, reaction_rate, lines, warp_matrix,
+        shear_rate, colour_weight.transpose(1, 2, 0).reshape(8, views), colour_bias.T, start, slab_order.T,
+        species, diffusivity, reaction_rate, owners[:, 0, :, 0], lengths[:, 0], warp_matrix,
     )
     return (species_out, frame.reshape(view_count, rows, 4, width))
 

time: 52.5 us -> 45.5 us (0.87)
  local copies, waits for them, and re-layouts: 8.53 us -> 3.27 us
  other arithmetic: 3.09 us -> 0.68 us
  Pallas kernels: 39.8 us -> 40.7 us
    unnamed x12 -> x6, local copies, waits for them, and re-layouts: 6.05 us -> 3.27 us
    another operation x4 -> x0, local copies, waits for them, and re-layouts: 1.54 us -> none  [the longest x2 0.77 us: body(): jnp.tile(owner, (1, 4))]
    mul x2 -> x0, other arithmetic: 1.46 us -> none  [the longest x1 0.8 us: body(): colour_weight * halves[None, :, None]]
    pallas_call x1, Pallas kernels: 39.8 us -> 40.7 us  [body(): pl.pallas_call(functools.partial(march_kernel, depth_devices, row_devices...]
    broadcast_in_dim x1 -> x0, local copies, waits for them, and re-layouts: 0.76 us -> none  [body(): jnp.repeat(owner, 4, axis=1)]
    sub x1 -> x0, other arithmetic: 0.73 us -> none  [body(): fraction = offset - floor_part]
where the time goes in v4:
time: 45.5 us; the launch traced here: 45.3 us
  Pallas kernels  40.7 us (89%)
  local copies, waits for them, and re-layouts  3.27 us (7%)
  other arithmetic  0.68 us (1%)
  between operations  0.67 us (1%)
    pallas_call x1, Pallas kernels, body(): pl.pallas_call(functools.partial(march_kernel, depth_devices, row_devices...  40.7 us
    unnamed x6, local copies, waits for them, and re-layouts  3.27 us

profile of v4, /device:TPU:0, one launch (start us, length us, event | category | flops | bytes accessed | tf_op | source)
XLA Modules:
  0.0 45.3 jit_solution(11653101302241195594)
XLA Ops:
  0.6 0.0 copy-start.1
  0.7 0.6 %copy-done.1 = f32[16]{0:T(128)S(1)} copy-done((f32[16]{0:T(128)S(1)}, f32[16]{0:T(128)}, u32[]{:S(2)}) %copy-start.1) | copy-done | bytes 88
  1.3 0.7 %add_clamp_fusion.start_ref = s32[16,16]{1,0:T(8,128)} fusion(f32[16]{0:T(128)S(1)} %convert_add_fusion, f32[16]{0:T(128)S(1)} %copy-done.1), kind=kLoop, calls=%fused_computation | loop fusion | flops 1280 | bytes 1152 | tf_op jit(solution)/shard_map/jit(clip)/min | solution.py:513
  2.0 40.7 %shard_map.113 = (f32[2,16,32,128]{3,2,1,0:T(8,128)}, f32[4,128,128]{2,1,0:T(8,128)}) custom-call(f32[16]{0:T(128)} %shear_ref.1, f32[8,16]{1,0:T(8,128)} %bitcast.9, f32[4,16]{1,0:T(4,128)} %bitcast.10, s32[16,16]{1,0:T(8,128)} %add_clamp_fusion.start_ref, s32[4,16]{1,0:T(4,128)} %bitcast.11, f32[2,16,32,128]{3,2,1,0:T(8,128)} %species_ref.1, ...), custom_call_target="tpu_custom_call" | custom-call | tf_op jit(solution)/shard_map/pallas_call | solution.py:518
  42.7 0.0 copy-start
  42.7 1.9 %copy.14 = f32[2,16,32,128]{3,2,1,0:T(8,128)} copy(f32[2,16,32,128]{3,2,1,0:T(8,128)} %get-tuple-element.8) | data formatting | bytes 1048576
  44.6 0.0 copy-done
  44.6 0.7 %copy.15 = f32[4,32,4,128]{3,2,1,0:T(4,128)} copy(f32[4,32,4,128]{3,2,1,0:T(4,128)S(1)} %bitcast.8) | data formatting | bytes 524288
  (1 shorter events, 0.0 us)
Async XLA Ops:
  0.6 0.7 %copy-start.1 = (f32[16]{0:T(128)S(1)}, f32[16]{0:T(128)}, u32[]{:S(2)}) copy-start(f32[16]{0:T(128)} %shear_ref.1) | copy-start | bytes 196
  42.7 1.9 %copy-start = (f32[4,128,128]{2,1,0:T(8,128)S(1)}, f32[4,128,128]{2,1,0:T(8,128)}, u32[]{:S(2)}) copy-start(f32[4,128,128]{2,1,0:T(8,128)} %get-tuple-element.5) | copy-start | bytes 786436

commit v5 on v4

--- a/solution.py
+++ b/solution.py
@@ -119,6 +119,19 @@
 
     lax.fori_loop(0, depth_cells, place_rows, 0)
 
+    lower = [(f, LAYERS + k, last + k) for f in range(2) for k in range(3)]
+    lower += [(f, LAYERS + k, last + k) for f in range(2, 4) for k in range(2)]
+    upper = [(f, last - 3 + k, k) for f in range(2) for k in range(3)]
+    upper += [(f, last - 3 + k, k) for f in range(2, 4) for k in range(1, 3)]
+    for way, items in enumerate((lower, upper)):
+        for pair in range(len(items) // 2):
+            planes = [deep[f, here, :, pl.ds(0, width)] for f, here, _ in items[2 * pair : 2 * pair + 2]]
+            stage_out[way, pair] = jnp.concatenate(planes, axis=0).astype(jnp.bfloat16)
+    body, rest = pl.ds(0, len(lower) // 2), pl.ds(len(lower) // 2, 1)
+    deep_down = [link(8, stage_out.at[0, body], stage_in.at[1, body], depth_down)]
+    deep_up = [link(9, stage_out.at[1, body], stage_in.at[0, body], depth_up)]
+    begin(me_d, depth_devices, deep_down, deep_up)
+
     lane = lax.broadcasted_iota(jnp.int32, (tall, width), 1)
 
     def turned(array, shift):
@@ -150,19 +163,12 @@
             jnp.where(lane >= width - edge, turned(below, width - edge - below_at), 0.0),
         )
 
-    lower = [(f, LAYERS + k, last + k) for f in range(2) for k in range(3)]
-    lower += [(f, LAYERS + k, last + k) for f in range(2, 4) for k in range(2)]
-    upper = [(f, last - 3 + k, k) for f in range(2) for k in range(3)]
-    upper += [(f, last - 3 + k, k) for f in range(2, 4) for k in range(1, 3)]
     span = 3 * edge
 
     def corner_at(field, side):
         return (field % 2) * (width // 2) + side * (width // 4)
 
     for way, (items, start) in enumerate(((lower, 0), (upper, edge * (depth_cells - 3)))):
-        for pair in range(len(items) // 2):
-            planes = [deep[f, here, :, pl.ds(0, width)] for f, here, _ in items[2 * pair : 2 * pair + 2]]
-            stage_out[way, pair] = jnp.concatenate(planes, axis=0).astype(jnp.bfloat16)
         corners = []
         for half in range(2):
             tile = jnp.zeros((tall, width), jnp.float32)
@@ -173,8 +179,8 @@
                     tile = jnp.where(here, turned(got[side, field], at - start), tile)
             corners.append(tile)
         stage_out[way, len(items) // 2] = jnp.concatenate(corners, axis=0).astype(jnp.bfloat16)
-    down = [link(8, stage_out.at[0], stage_in.at[1], depth_down)]
-    up = [link(9, stage_out.at[1], stage_in.at[0], depth_up)]
+    down = [link(10, stage_out.at[0, rest], stage_in.at[1, rest], depth_down)]
+    up = [link(11, stage_out.at[1, rest], stage_in.at[0, rest], depth_up)]
     begin(me_d, depth_devices, down, up)
 
     def place_sides(field, carry):
@@ -250,7 +256,7 @@
     inner(first_stage, LAYERS + 1, last - 1)
     inner(second_stage, LAYERS + 2, last - 2)
     inner(third_stage, LAYERS + 3, last - 3)
-    finish(me_d, depth_devices, down, up, stage_in.at[0], stage_in.at[1])
+    finish(me_d, depth_devices, deep_down + down, deep_up + up, stage_in.at[0], stage_in.at[1])
     for way, (items, place) in enumerate(((upper, 0), (lower, last))):
         pairs = len(items) // 2
         corners = stage_in[way, pairs].astype(jnp.float32)
@@ -379,7 +385,7 @@
 
         zero = jnp.zeros((rows, width), jnp.float32)
         red, green, blue, through = lax.fori_loop(
-            0, depth_cells, cells, (zero, zero, zero, zero + 1.0), unroll=4
+            0, depth_cells, cells, (zero, zero, zero, zero + 1.0), unroll=8
         )
         opacity = 1.0 - through
         for channel, value in enumerate((red, green, blue, opacity)):
@@ -553,8 +559,8 @@
             pltpu.VMEM((2, 4, tall, width), jnp.float32),
             pltpu.VMEM((2, 6, 2 * tall, width), jnp.bfloat16),
             pltpu.VMEM((2, 6, 2 * tall, width), jnp.bfloat16),
-            pltpu.SemaphoreType.DMA((10,)),
-            pltpu.SemaphoreType.DMA((10,)),
+            pltpu.SemaphoreType.DMA((12,)),
+            pltpu.SemaphoreType.DMA((12,)),
         ],
         compiler_params=pltpu.CompilerParams(
             collective_id=1, has_side_effects=True, vmem_limit_bytes=60 * 1024 * 1024

time: 45.5 us -> 45.3 us (level)
  no operation moved by 1% of the time
where the time goes in v5:
time: 45.3 us; the launch traced here: 45.1 us
  Pallas kernels  40.5 us (89%)
  local copies, waits for them, and re-layouts  3.27 us (7%)
  other arithmetic  0.68 us (2%)
  between operations  0.67 us (1%)
    pallas_call x1, Pallas kernels, body(): pl.pallas_call(functools.partial(march_kernel, depth_devices, row_devices...  40.5 us
    unnamed x6, local copies, waits for them, and re-layouts  3.27 us

profile of v5, /device:TPU:0, one launch (start us, length us, event | category | flops | bytes accessed | tf_op | source)
XLA Modules:
  0.0 45.1 jit_solution(12191122612985195100)
XLA Ops:
  0.6 0.0 copy-start.1
  0.7 0.6 %copy-done.1 = f32[16]{0:T(128)S(1)} copy-done((f32[16]{0:T(128)S(1)}, f32[16]{0:T(128)}, u32[]{:S(2)}) %copy-start.1) | copy-done | bytes 88
  1.3 0.7 %add_clamp_fusion.start_ref = s32[16,16]{1,0:T(8,128)} fusion(f32[16]{0:T(128)S(1)} %convert_add_fusion, f32[16]{0:T(128)S(1)} %copy-done.1), kind=kLoop, calls=%fused_computation | loop fusion | flops 1280 | bytes 1152 | tf_op jit(solution)/shard_map/jit(clip)/min | solution.py:519
  2.0 40.5 %shard_map.113 = (f32[2,16,32,128]{3,2,1,0:T(8,128)}, f32[4,128,128]{2,1,0:T(8,128)}) custom-call(f32[16]{0:T(128)} %shear_ref.1, f32[8,16]{1,0:T(8,128)} %bitcast.9, f32[4,16]{1,0:T(4,128)} %bitcast.10, s32[16,16]{1,0:T(8,128)} %add_clamp_fusion.start_ref, s32[4,16]{1,0:T(4,128)} %bitcast.11, f32[2,16,32,128]{3,2,1,0:T(8,128)} %species_ref.1, ...), custom_call_target="tpu_custom_call" | custom-call | tf_op jit(solution)/shard_map/pallas_call | solution.py:524
  42.5 0.0 copy-start
  42.5 1.9 %copy.14 = f32[2,16,32,128]{3,2,1,0:T(8,128)} copy(f32[2,16,32,128]{3,2,1,0:T(8,128)} %get-tuple-element.8) | data formatting | bytes 1048576
  44.4 0.0 copy-done
  44.4 0.7 %copy.15 = f32[4,32,4,128]{3,2,1,0:T(4,128)} copy(f32[4,32,4,128]{3,2,1,0:T(4,128)S(1)} %bitcast.8) | data formatting | bytes 524288
  (1 shorter events, 0.0 us)
Async XLA Ops:
  0.6 0.7 %copy-start.1 = (f32[16]{0:T(128)S(1)}, f32[16]{0:T(128)}, u32[]{:S(2)}) copy-start(f32[16]{0:T(128)} %shear_ref.1) | copy-start | bytes 196
  42.5 1.9 %copy-start = (f32[4,128,128]{2,1,0:T(8,128)S(1)}, f32[4,128,128]{2,1,0:T(8,128)}, u32[]{:S(2)}) copy-start(f32[4,128,128]{2,1,0:T(8,128)} %get-tuple-element.5) | copy-start | bytes 786436
